TPU v7x, 256 devices: a whole 4x4x8 slice. The times are simulated.
256 devices in a mesh: loop: 8 (over x_lo, y), dp: 32 (over x_hi, z, core).
Axes of the slice: x: 4 (x_hi: 2, x_lo: 2; x = x_hi * 2 + x_lo), y: 4, z: 8, core: 2. Of those that a mesh axis runs over, the one named last changes fastest.
Arguments:
- residual: bfloat16 [12288, 1024], P('dp', 'loop'), may hold values from -6 to 6
- targets: bfloat16 [12288, 2, 1024], P('dp'), may hold values from -6 to 6
- counts: int32 [32], P('dp'), may hold values from 1 to 384, 6144 in all
- enc_weight: bfloat16 [1024, 16384], P('dp', 'loop'), may hold values from -0.1875 to 0.1875
- enc_bias: float32 [16384], P('loop'), may hold values from -3 to 3
- dec_weight: bfloat16 [16384, 2, 1024], P(('loop', 'dp')), may hold values from -0.046875 to 0.046875
Outputs:
- mean_error: float32 [], replicated
- enc_grad: float32 [1024, 16384], P('dp', 'loop')
- bias_grad: float32 [16384], P('loop')
- dec_grad: float32 [16384, 2, 1024], P(('loop', 'dp'))
Inputs may be any that keep to these rules, and one draw needn't show every extreme that they name: The 32 counts sum to 6144, and the largest is 384.
All inputs are finite; a program needn't handle non-finite values. No bound on the sum of `counts` on one device may be relied on, other than what follows from the above.
Results may differ from a plain program's by a relative error of at most 0.022.
Values may be sent and summed in bfloat16 or wider, within the bound.
A program may use at most 128 MiB of HBM per device.

v0:
```python
import math

import jax
import jax.numpy as jnp
from jax import lax
from jax.sharding import PartitionSpec as P


def shards(residual, targets, counts, enc_weight, enc_bias, dec_weight):
    row_count = residual.shape[0]
    parts = targets.shape[1]
    features_all = lax.all_gather(residual, "loop", axis=1, tiled=True)
    d_model = features_all.shape[1]
    latents = enc_weight.shape[1]
    feature_cols = features_all
    preact = jnp.dot(
        feature_cols,
        lax.all_gather(enc_weight, "dp", axis=0, tiled=True),
        preferred_element_type=jnp.float32,
    )
    preact = preact + enc_bias[None, :]
    active = jnp.maximum(preact, 0.0).astype(jnp.bfloat16)
    decoder = lax.all_gather(dec_weight, "dp", axis=0, tiled=True)
    dec_flat = decoder.reshape(latents, parts * d_model)
    partial_value = jnp.dot(active, dec_flat, preferred_element_type=jnp.float32).reshape(
        row_count, parts, d_model
    )
    total_rows = lax.axis_size("dp") * row_count // 2
    grad_scale = 2.0 / math.sqrt(total_rows)
    row_valid = (lax.iota(jnp.int32, row_count) < counts[0]).astype(jnp.float32)[:, None, None]
    rebuilt = lax.psum(partial_value.astype(jnp.bfloat16), "loop").astype(jnp.float32)
    misfit = (rebuilt - targets.astype(jnp.float32)) * row_valid
    sq_total = lax.psum(jnp.sum(misfit * misfit), "dp")
    out_grad = (grad_scale * misfit).astype(jnp.bfloat16)
    mean_error = sq_total / (total_rows * parts * d_model)
    grad_flat = out_grad.reshape(row_count, parts * d_model)
    backprop = lax.dot_general(
        grad_flat, dec_flat, (((1,), (1,)), ((), ())), preferred_element_type=jnp.float32
    )
    pre_grad = jnp.where(preact > 0, backprop, 0.0)
    bias_grad = lax.psum(jnp.sum(pre_grad, axis=0), "dp")
    pre_narrow = pre_grad.astype(jnp.bfloat16)
    product = lax.dot_general(
        active, grad_flat, (((0,), (0,)), ((), ())), preferred_element_type=jnp.float32
    )
    dec_grad = lax.psum_scatter(
        product.reshape(lax.axis_size("dp") * dec_weight.shape[0], parts, d_model).astype(
            jnp.bfloat16
        ),
        "dp",
        scatter_dimension=0,
        tiled=True,
    ).astype(jnp.float32)
    feature_cols = features_all
    enc_grad = lax.psum_scatter(
        lax.dot_general(
            feature_cols, pre_narrow, (((0,), (0,)), ((), ())), preferred_element_type=jnp.float32
        ).astype(jnp.bfloat16),
        "dp",
        scatter_dimension=0,
        tiled=True,
    ).astype(jnp.float32)
    return (mean_error, enc_grad, bias_grad, dec_grad)


def solution(mesh):
    placed = (
        P("dp", "loop"),
        P("dp", None, None),
        P("dp"),
        P("dp", "loop"),
        P("loop"),
        P(("loop", "dp"), None, None),
    )
    return jax.shard_map(
        shards,
        mesh=mesh,
        in_specs=placed,
        out_specs=(P(), P("dp", "loop"), P("loop"), P(("loop", "dp"), None, None)),
        check_vma=False,
    )
```

profile of v0, /device:TPU:1, one launch (start us, length us, event | category | flops | bytes accessed | tf_op | source)
XLA Modules:
  0.0 615.8 jit_solution(3905946032527150513)
XLA Ops:
  7.2 0.0 all-gather.3.cloned.1.call-start
  7.2 0.7 all-gather.3.cloned.1.call-update
  7.9 0.0 all-gather.5.cloned.1.call-start
  7.9 1.7 copy.22
  9.7 0.0 all-gather.5.cloned.1.call-update
  9.7 0.0 all-reduce.3.cloned.1.call-start
  9.7 26.4 %all_gather.9 = bf16[384,1024]{1,0:T(8,128)(2,1)S(1)} all-gather(bf16[384,128]{1,0:T(8,128)(2,1)} %param.6), channel_id=1, replica_groups=mesh['loop'=8,'dp'=32] {'loop'}, dimensions={1}, use_global_device_ids=true | all-gather | bytes 884736 | tf_op jit(solution)/shard_map/all_gather | solution.py:12
  36.1 65.7 %all-gather.3.cloned.1.call-done = bf16[1024,2048]{1,0:T(8,128)(2,1)} async-done(((bf16[32,2048]{1,0:T(8,128)(2,1)}), bf16[1024,2048]{1,0:T(8,128)(2,1)}) %all-gather.3.cloned.1.call-update) | async-done | bytes 4194320 | tf_op jit(solution)/shard_map/all_gather | solution.py:18
  101.8 5.6 fusion.14
  107.4 0.0 copy-done.1
  107.4 95.9 %all-gather.5.cloned.1.call-done = bf16[2048,2,1024]{2,0,1:T(8,128)(2,1)} async-done(((bf16[64,2,1024]{2,0,1:T(8,128)(2,1)}), bf16[2048,2,1024]{2,0,1:T(8,128)(2,1)}) %all-gather.5.cloned.1.call-update) | async-done | bytes 8388624 | tf_op jit(solution)/shard_map/all_gather | solution.py:23
  203.3 11.7 %copy.23 = bf16[2048,2,1024]{0,2,1:T(8,128)(2,1)} copy(bf16[2048,2,1024]{2,0,1:T(8,128)(2,1)} %all-gather.5.cloned.1.call-done) | data formatting | bytes 16777216 | tf_op jit(solution)/shard_map/all_gather | solution.py:23
  215.1 0.0 copy-done.3
  215.1 9.1 %fusion.2 = bf16[384,2,1024]{2,0,1:T(8,128)(2,1)} fusion(bf16[2048,2,1024]{0,2,1:T(8,128)(2,1)} %copy.23, f32[384,2048]{1,0:T(8,128)} %fusion.14, f32[2048]{0:T(1024)S(1)} %copy-done.3), kind=kOutput, calls=%fused_computation.9 | convolution fusion | flops 3224371200 | bytes 13115392 | tf_op jit(solution)/shard_map/dot_general | solution.py:25
  224.1 0.0 all-reduce.3.cloned.1.call-update
  224.1 0.2 reduce-scatter.7.cloned.1.call-start
  225.0 75.8 %all-reduce.3.cloned.1.call-done = bf16[384,2,1024]{2,0,1:T(8,128)(2,1)} async-done(((bf16[384,2,1024]{2,0,1:T(8,128)(2,1)}), bf16[384,2,1024]{2,0,1:T(8,128)(2,1)}) %all-reduce.3.cloned.1.call-update) | async-done | bytes 1572880 | tf_op jit(solution)/shard_map/psum | solution.py:31
  300.8 3.2 multiply_convert_fusion
  304.0 7.0 %fusion.13 = (f32[2048]{0:T(1024)S(1)}, bf16[384,2048]{1,0:T(8,128)(2,1)S(1)}) fusion(bf16[384,2,1024]{2,0,1:T(8,128)(2,1)S(1)} %get-tuple-element.18, bf16[2048,2,1024]{2,0,1:T(8,128)(2,1)} %all-gather.5.cloned.1.call-done, f32[384,2048]{1,0:T(8,128)S(1)} %copy-done.4, f32[2048]{0:T(1024)S(1)} %copy-done.3), kind=kOutput, calls=%fused_computation.17 | convolution fusion | flops 3225155584 | bytes 14696448 | tf_op jit(solution)/shard_map/dot_general | solution.py:37
  311.0 4.3 convert_bitcast_fusion
  315.4 6.5 %copy.31 = bf16[1024,2048]{1,0:T(8,128)(2,1)} copy(bf16[1024,2048]{0,1:T(8,128)(2,1)} %convert_bitcast_fusion) | data formatting | bytes 8388608
  321.8 0.0 reduce-scatter.7.cloned.1.call-update
  321.9 0.0 reduce-scatter.5.cloned.1.call-start
  321.9 0.9 copy.25
  322.8 8.8 %convolution_convert_fusion = bf16[2048,2,1024]{2,0,1:T(8,128)(2,1)} fusion(bf16[384,2,1024]{0,2,1:T(8,128)(2,1)S(1)} %copy.25, f32[384,2048]{1,0:T(8,128)} %fusion.14, f32[2048]{0:T(1024)S(1)} %copy-done.3), kind=kOutput, calls=%fused_computation.2 | convolution fusion | flops 3227779072 | bytes 13115392 | tf_op jit(solution)/shard_map/dot_general | solution.py:43
  331.6 0.0 reduce-scatter.5.cloned.1.call-update
  331.6 72.6 %all-reduce = (f32[]{:T(128)}, f32[2048]{0:T(1024)}) all-reduce(f32[]{:T(128)} %get-tuple-element.19, f32[2048]{0:T(1024)S(1)} %get-tuple-element.20), channel_id=1, replica_groups=mesh['loop'=8,'dp'=32] {'dp'}, use_global_device_ids=true, to_apply=%region_2.0 | all-reduce | flops 2049 | bytes 16392 | tf_op jit(solution)/shard_map/psum | solution.py:33
  404.9 44.6 %reduce-scatter.7.cloned.1.call-done = bf16[32,2048]{1,0:T(8,128)(2,1)} async-done(((bf16[1024,2048]{1,0:T(8,128)(2,1)}), bf16[32,2048]{1,0:T(8,128)(2,1)}) %reduce-scatter.7.cloned.1.call-update) | async-done | bytes 131088
  449.5 1.2 copy.32
  450.7 0.9 copy.27
  451.6 154.5 %reduce-scatter.5.cloned.1.call-done = bf16[64,2,1024]{2,0,1:T(8,128)(2,1)} async-done(((bf16[2048,2,1024]{2,0,1:T(8,128)(2,1)}), bf16[64,2,1024]{2,0,1:T(8,128)(2,1)}) %reduce-scatter.5.cloned.1.call-update) | async-done | bytes 262160 | tf_op jit(solution)/shard_map/reduce_scatter | solution.py:46
  606.1 2.0 copy.28
  (9 shorter events, 0.0 us)
Async XLA Ops:
  7.2 94.6 %all-gather.3.cloned.1.call-start = ((), (), s32[]{:S(2)}) async-start(), calls=%async_computation.2 | async-start | bytes 4325376 | tf_op jit(solution)/shard_map/all_gather | solution.py:18
  7.9 195.4 %all-gather.5.cloned.1.call-start = ((), (), s32[]{:S(2)}) async-start(), calls=%async_computation.3 | async-start | bytes 8650752 | tf_op jit(solution)/shard_map/all_gather | solution.py:23
  9.7 291.1 %all-reduce.3.cloned.1.call-start = ((), (), s32[]{:S(2)}) async-start(), calls=%async_computation.4 | async-start | bytes 3145728 | tf_op jit(solution)/shard_map/psum | solution.py:31
  36.1 71.3 %copy-start.1 = (bf16[384,1024]{1,0:T(8,128)(2,1)}, bf16[384,1024]{1,0:T(8,128)(2,1)S(1)}, u32[]{:S(2)}) copy-start(bf16[384,1024]{1,0:T(8,128)(2,1)S(1)} %all_gather.9) | copy-start | bytes 2359300
  107.4 107.6 %copy-start.3 = (f32[2048]{0:T(1024)S(1)}, f32[2048]{0:T(1024)}, u32[]{:S(2)}) copy-start(f32[2048]{0:T(1024)} %param.10) | copy-start | bytes 24580
  215.1 85.8 %copy-start = (bf16[384,2,1024]{2,1,0:T(2,128)(2,1)S(1)}, bf16[384,2,1024]{2,1,0:T(2,128)(2,1)}, u32[]{:S(2)}) copy-start(bf16[384,2,1024]{2,1,0:T(2,128)(2,1)} %param.7) | copy-start | bytes 4718596
  224.1 225.3 %reduce-scatter.7.cloned.1.call-start = ((), (), s32[]{:S(2)}) async-start(), calls=%async_computation.6 | async-start | bytes 4325376
  300.8 3.2 copy-start.4
  304.0 7.0 %copy-start.2 = (bf16[384,1024]{1,0:T(8,128)(2,1)S(1)}, bf16[384,1024]{1,0:T(8,128)(2,1)}, u32[]{:S(2)}) copy-start(bf16[384,1024]{1,0:T(8,128)(2,1)} %copy-done.1) | copy-start | bytes 2359300
  321.9 284.2 %reduce-scatter.5.cloned.1.call-start = ((), (), s32[]{:S(2)}) async-start(), calls=%async_computation.5 | async-start | bytes 8650752 | tf_op jit(solution)/shard_map/reduce_scatter | solution.py:46
Sparse Core Ops, SparseCore 0:
  10.8 90.9 all-gather.2
  105.2 98.1 all-gather.4
  224.3 76.5 all-reduce.2
  322.0 127.4 reduce-scatter.6
  454.4 151.6 reduce-scatter.4
where the time goes:
time: 620 us; the launch traced here: 616 us
  waiting for transfers between devices  437 us (70%)
  blocking collectives  99 us (16%)
  matrix products  34.8 us (6%)
  local copies, waits for them, and re-layouts  24.8 us (4%)
  between operations  16.3 us (3%)
    reduce_scatter x1, waiting for transfers between devices, shards(): lax.psum_scatter(product.reshape(lax.axis_size('dp') * dec_weight.shape[0...  155 us
    all_gather x1, waiting for transfers between devices, shards(): decoder = lax.all_gather(dec_weight, 'dp', axis=0, tiled=True)  95.9 us
    psum x1, waiting for transfers between devices, shards(): lax.psum(partial_value.astype(jnp.bfloat16), 'loop').astype(jnp.float32)  75.8 us
    psum x1, blocking collectives, shards(): sq_total = lax.psum(jnp.sum(misfit * misfit), 'dp')  72.6 us
    all_gather x1, waiting for transfers between devices, shards(): lax.all_gather(enc_weight, 'dp', axis=0, tiled=True)  65.7 us
    unnamed x6, waiting for transfers between devices  45.4 us
    all_gather x1, blocking collectives, shards(): features_all = lax.all_gather(residual, 'loop', axis=1, tiled=True)  26.4 us
  transfers between devices with their start and end apart: 5, of which 5 were waited for; matrix products, arithmetic and copies ran while one was open for 3% of the time, Pallas kernels for 0%

commit v1 on v0

v1 whole, which is shorter than its diff:
```python
import math

import jax
import jax.numpy as jnp
from jax import lax
from jax.experimental import pallas as pl
from jax.experimental.pallas import tpu as pltpu
from jax.sharding import PartitionSpec as P

MESH = pl.DeviceIdType.MESH
BF16 = jnp.bfloat16
F32 = jnp.float32


def place():
    loop, dp = lax.axis_index("loop"), lax.axis_index("dp")
    x = (dp // 16) * 2 + loop // 4
    return x, loop % 4, (dp % 16) // 2, dp % 2


def ident(x, y, z, core):
    return ((x % 2) * 4 + y, (x // 2) * 16 + z * 2 + core)


def greet(peers):
    barrier = pltpu.get_barrier_semaphore()
    for peer in peers:
        pl.semaphore_signal(barrier, inc=1, device_id=peer, device_id_type=MESH)
    pl.semaphore_wait(barrier, len(peers))


def remote(src, dst, send, recv, peer):
    return pltpu.make_async_remote_copy(
        src_ref=src, dst_ref=dst, send_sem=send, recv_sem=recv, device_id=peer, device_id_type=MESH
    )


class Gather:
    def __init__(self, n, at, right, left, whole, half, sems):
        self.n, self.at, self.right, self.left = n, at, right, left
        self.whole, self.half, self.sems = whole, half, sems
        self.steps = []

    def step(self):
        s = len(self.steps)
        if s:
            for copy in self.steps[-1]:
                copy.wait_recv()
        if s == self.n // 2:
            return
        pair = []
        for side, peer in ((0, self.right), (1, self.left)):
            block = (self.at + (self.n - s if side == 0 else s)) % self.n
            ref = self.half(block, side) if s == self.n // 2 - 1 else self.whole(block)
            copy = remote(ref, ref, self.sems.at[0, side, s], self.sems.at[1, side, s], peer)
            copy.start()
            pair.append(copy)
        self.steps.append(pair)

    def drain(self):
        for pair in self.steps:
            for copy in pair:
                copy.wait_send()


def add_into(ref, other):
    ref[...] = (ref[...].astype(F32) + other[...].astype(F32)).astype(BF16)


class Reduce:
    def __init__(self, n, at, right, left, whole, half, landed, sems):
        self.n, self.at, self.right, self.left = n, at, right, left
        self.whole, self.half, self.landed, self.sems = whole, half, landed, sems
        self.steps = []

    def step(self):
        s = len(self.steps)
        depth = self.n // 2
        pair = []
        for side, peer in ((0, self.right), (1, self.left)):
            if s:
                self.steps[-1][side].wait_recv()
            if s == depth:
                continue
            far = depth - s
            block = (self.at + (far if side == 0 else self.n - far)) % self.n
            if s:
                part = self.half(block, side) if s == 1 else self.whole(block)
                add_into(part, self.landed[side][s - 1])
            ref = self.half(block, side) if s == 0 else self.whole(block)
            copy = remote(ref, self.landed[side][s], self.sems.at[0, side, s], self.sems.at[1, side, s], peer)
            copy.start()
            pair.append(copy)
        if s < depth:
            self.steps.append(pair)

    def drain(self):
        for pair in self.steps:
            for copy in pair:
                copy.wait_send()


def gather_kernel(res, enc, dec, res_all, enc_all, dec_all, ysem, xsem, esem, dsem, qsem, csem, lsem):
    x, y, z, core = place()
    x_hi = x // 2
    up, down = ident(x, y, (z + 1) % 8, core), ident(x, y, (z + 7) % 8, core)
    east, west = ident((x + 1) % 4, y, z, core), ident((x + 3) % 4, y, z, core)
    north, south = ident(x, (y + 1) % 4, z, core), ident(x, (y + 3) % 4, z, core)
    other = ident(x, y, z, 1 - core)
    quad = [(1 - x_hi, core), (x_hi, 1 - core), (1 - x_hi, 1 - core)]
    quad_ids = [ident((x + 2) % 4, y, z, core), other, ident((x + 2) % 4, y, z, 1 - core)]
    greet([up, down, east, west, north, south] + quad_ids)

    def cols(block, width):
        return pl.ds(pl.multiple_of(block * width, width), width)

    def mine(xx, yy):
        return res_all.at[core, xx // 2, :, cols((xx % 2) * 4 + yy, 128)]

    local = [
        pltpu.make_async_copy(res, mine(x, y), lsem.at[0]),
        pltpu.make_async_copy(enc.at[x_hi, core], enc_all.at[x_hi, z, core], lsem.at[1]),
        pltpu.make_async_copy(dec, dec_all.at[z], lsem.at[2]),
    ]
    for copy in local:
        copy.start()
    swap = []
    for i, (q, peer) in enumerate(zip(quad, quad_ids)):
        copy = remote(enc.at[q[0], q[1]], enc_all.at[x_hi, z, core], qsem.at[0, i], qsem.at[1, i], peer)
        copy.start()
        swap.append(copy)
    for copy in local:
        copy.wait()
    ring_y = Gather(
        4, y, north, south, lambda b: mine(x, b),
        lambda b, h: res_all.at[core, x_hi, pl.ds(192 * h, 192), cols((x % 2) * 4 + b, 128)], ysem,
    )
    ring_x = Gather(
        4, x, east, west, lambda b: res_all.at[core, b // 2, :, cols(b % 2, 512)],
        lambda b, h: res_all.at[core, b // 2, pl.ds(192 * h, 192), cols(b % 2, 512)], xsem,
    )
    ring_e = Gather(8, z, up, down, lambda b: enc_all.at[:, b], lambda b, h: enc_all.at[h, b], esem)
    ring_d = Gather(8, z, up, down, lambda b: dec_all.at[b], lambda b, h: dec_all.at[b, pl.ds(32 * h, 32)], dsem)
    ring_y.step()
    for copy in swap:
        copy.wait_recv()
    ring_e.step()
    ring_d.step()
    ring_y.step()
    ring_y.step()
    ring_x.step()
    ring_e.step()
    ring_d.step()
    ring_x.step()
    ring_e.step()
    ring_d.step()
    ring_x.step()
    cross = remote(res_all.at[core], res_all.at[core], csem.at[0], csem.at[1], other)
    cross.start()
    ring_e.step()
    ring_d.step()
    ring_e.step()
    ring_d.step()
    cross.wait()
    for copy in swap:
        copy.wait_send()
    for ring in (ring_y, ring_x, ring_e, ring_d):
        ring.drain()


def exchange_kernel(
    scale, part, goal, valid, grads, sq, crossed,
    a1, a2, b1, b2, c1, c2, d1, d2, mid_a, mid_b,
    asem, bsem, csem, dsem, esem, fsem, gsem, hsem, osem,
):
    x, y, z, core = place()
    east, west = ident((x + 1) % 4, y, z, core), ident((x + 3) % 4, y, z, core)
    north, south = ident(x, (y + 1) % 4, z, core), ident(x, (y + 3) % 4, z, core)
    other = ident(x, y, z, 1 - core)
    greet([east, west, north, south, other])
    lo, hi = pl.ds(0, 1024), pl.ds(1024, 1024)
    cross = remote(part.at[1 - core], crossed, osem.at[0, 0], osem.at[0, 1], other)
    cross.start()
    cross.wait()
    mine = part.at[core]

    def total(i, _):
        add_into(mine.at[i // 4, i % 4], crossed.at[i // 4, i % 4])
        return 0

    lax.fori_loop(0, 16, total, 0)
    red_a = Reduce(
        4, x, east, west, lambda b: mine.at[b, :, :, lo], lambda b, h: mine.at[b, pl.ds(2 * h, 2), :, lo],
        [[a1.at[s], a2.at[s]] for s in range(2)], asem,
    )
    red_b = Reduce(
        4, y, north, south, lambda b: mine.at[:, b, :, hi], lambda b, h: mine.at[pl.ds(2 * h, 2), b, :, hi],
        [[b1.at[s], b2.at[s]] for s in range(2)], bsem,
    )
    for _ in range(3):
        red_a.step()
        red_b.step()
    mid_a[...] = (mine[x, :, :, lo].astype(F32) + a2[0].astype(F32) + a2[1].astype(F32)).astype(BF16)
    red_c = Reduce(
        4, y, north, south, lambda b: mid_a.at[b], lambda b, h: mid_a.at[b, :, pl.ds(512 * h, 512)],
        [[c1.at[s], c2.at[s]] for s in range(2)], csem,
    )
    red_c.step()
    mid_b[...] = (mine[:, y, :, hi].astype(F32) + b2[0].astype(F32) + b2[1].astype(F32)).astype(BF16)
    red_d = Reduce(
        4, x, east, west, lambda b: mid_b.at[b], lambda b, h: mid_b.at[b, :, pl.ds(512 * h, 512)],
        [[d1.at[s], d2.at[s]] for s in range(2)], dsem,
    )
    red_d.step()
    for _ in range(2):
        red_c.step()
        red_d.step()
    out = grads.at[core]
    ok = valid[:, 0:1]
    rebuilt = mid_a[y].astype(F32) + c2[0].astype(F32) + c2[1].astype(F32)
    miss = (rebuilt - goal[:, lo].astype(F32)) * ok
    out[x, y, :, lo] = (scale * miss).astype(BF16)
    squares = jnp.sum(miss * miss, axis=0, keepdims=True)
    ring_c = Gather(
        4, y, north, south, lambda b: out.at[x, b, :, lo], lambda b, h: out.at[x, b, :, pl.ds(512 * h, 512)], esem
    )
    ring_c.step()
    rebuilt = mid_b[x].astype(F32) + d2[0].astype(F32) + d2[1].astype(F32)
    miss = (rebuilt - goal[:, hi].astype(F32)) * ok
    out[x, y, :, hi] = (scale * miss).astype(BF16)
    squares = squares + jnp.sum(miss * miss, axis=0, keepdims=True)
    ring_d = Gather(
        4, x, east, west, lambda b: out.at[b, y, :, hi],
        lambda b, h: out.at[b, y, :, pl.ds(1024 + 512 * h, 512)], fsem,
    )
    ring_d.step()
    sq[...] = squares
    for _ in range(2):
        ring_c.step()
        ring_d.step()
    ring_a = Gather(
        4, x, east, west, lambda b: out.at[b, :, :, lo], lambda b, h: out.at[b, pl.ds(2 * h, 2), :, lo], gsem
    )
    ring_b = Gather(
        4, y, north, south, lambda b: out.at[:, b, :, hi], lambda b, h: out.at[pl.ds(2 * h, 2), b, :, hi], hsem
    )
    for _ in range(3):
        ring_a.step()
        ring_b.step()
    back = remote(out, out, osem.at[1, 0], osem.at[1, 1], other)
    back.start()
    for ring in (red_a, red_b, red_c, red_d, ring_a, ring_b, ring_c, ring_d):
        ring.drain()
    back.wait()


def scatter_kernel(dec, enc, dec_out, enc_out, d1, dn, e1, en, dsem, esem, esum, qsem, lsem):
    x, y, z, core = place()
    x_hi = x // 2
    up, down = ident(x, y, (z + 1) % 8, core), ident(x, y, (z + 7) % 8, core)
    quad = [(1 - x_hi, core), (x_hi, 1 - core), (1 - x_hi, 1 - core)]
    quad_ids = [
        ident((x + 2) % 4, y, z, core), ident(x, y, z, 1 - core), ident((x + 2) % 4, y, z, 1 - core)
    ]
    greet([up, down] + quad_ids)
    red_d = Reduce(
        8, z, up, down, lambda b: dec.at[b], lambda b, h: dec.at[b, pl.ds(32 * h, 32)],
        [[d1.at[s], dn.at[s, 0], dn.at[s, 1], dn.at[s, 2]] for s in range(2)], dsem,
    )
    red_e = Reduce(
        8, z, up, down, lambda b: enc.at[:, b], lambda b, h: enc.at[h, b],
        [[e1.at[s], en.at[s, 0], en.at[s, 1], en.at[s, 2]] for s in range(2)], esem,
    )
    for _ in range(5):
        red_e.step()
        red_d.step()
    esum[...] = enc[:, z].astype(F32) + en[0, 2].astype(F32) + en[1, 2].astype(F32)
    keep = pltpu.make_async_copy(esum.at[x_hi, core], enc_out.at[x_hi, core], lsem.at[0])
    keep.start()
    swap = []
    for i, (q, peer) in enumerate(zip(quad, quad_ids)):
        copy = remote(esum.at[q[0], q[1]], enc_out.at[x_hi, core], qsem.at[0, i], qsem.at[1, i], peer)
        copy.start()
        swap.append(copy)
    dec_out[...] = dec[z].astype(F32) + dn[0, 2].astype(F32) + dn[1, 2].astype(F32)
    keep.wait()
    for copy in swap:
        copy.wait()
    red_d.drain()
    red_e.drain()


VM = pl.BlockSpec(memory_space=pltpu.VMEM)


def dmas(*shape):
    return pltpu.SemaphoreType.DMA(shape)


def params(ident):
    return pltpu.CompilerParams(collective_id=ident, has_side_effects=True, vmem_limit_bytes=56 << 20)


def shape(*dims, dtype=BF16):
    return jax.ShapeDtypeStruct(dims, dtype)


def shards(residual, targets, counts, enc_weight, enc_bias, dec_weight):
    loop, dp = lax.axis_index("loop"), lax.axis_index("dp")
    x_hi, core = dp // 16, dp % 2
    enc_quad = enc_weight.reshape(32, 2, 8, 2, 64).transpose(1, 3, 0, 2, 4).reshape(2, 2, 32, 512)
    res_all, enc_all, dec_all = pl.pallas_call(
        gather_kernel,
        out_shape=(shape(2, 2, 384, 1024), shape(2, 8, 2, 32, 512), shape(8, 64, 2048)),
        in_specs=[VM] * 3,
        out_specs=(VM,) * 3,
        scratch_shapes=[dmas(2, 2, 2), dmas(2, 2, 2), dmas(2, 2, 4), dmas(2, 2, 4), dmas(2, 3), dmas(2), dmas(3)],
        compiler_params=params(1),
    )(residual, enc_quad, dec_weight.reshape(64, 2048))
    feats = res_all.reshape(1536, 1024)
    enc = enc_all.reshape(1024, 512)
    dec = dec_all.reshape(512, 2048)
    bias = lax.dynamic_index_in_dim(
        enc_bias.reshape(2, 8, 2, 64).transpose(0, 2, 1, 3).reshape(4, 512), x_hi * 2 + core, 0, False
    )
    preact = jnp.dot(feats, enc, preferred_element_type=F32) + bias[None, :]
    active = jnp.maximum(preact, 0.0).astype(BF16)
    part = jnp.dot(active, dec, preferred_element_type=F32).astype(BF16)
    goal = lax.dynamic_slice_in_dim(targets, loop * 48, 48, 0).reshape(48, 2048)
    rows = loop * 48 + lax.iota(jnp.int32, 48)
    valid = jnp.broadcast_to((rows < counts[0]).astype(F32)[:, None], (48, 128))
    total_rows = 32 * 384 // 2
    quarter = (2, 2, 48, 1024)
    whole = (2, 4, 48, 1024)
    grads, sq = pl.pallas_call(
        lambda *refs: exchange_kernel(2.0 / math.sqrt(total_rows), *refs),
        out_shape=(shape(2, 4, 4, 48, 2048), shape(1, 1024, dtype=F32)),
        in_specs=[VM] * 3,
        out_specs=(VM,) * 2,
        scratch_shapes=[
            pltpu.VMEM((4, 4, 48, 2048), BF16),
            pltpu.VMEM(quarter, BF16), pltpu.VMEM(whole, BF16),
            pltpu.VMEM(quarter, BF16), pltpu.VMEM(whole, BF16),
            pltpu.VMEM((2, 48, 512), BF16), pltpu.VMEM((2, 48, 1024), BF16),
            pltpu.VMEM((2, 48, 512), BF16), pltpu.VMEM((2, 48, 1024), BF16),
            pltpu.VMEM((4, 48, 1024), BF16), pltpu.VMEM((4, 48, 1024), BF16),
        ] + [dmas(2, 2, 2)] * 8 + [dmas(2, 2)],
        compiler_params=params(2),
    )(part.reshape(2, 4, 4, 48, 2048), goal, valid)
    mean_error = lax.psum(jnp.sum(sq), ("loop", "dp")) / (total_rows * 2048)
    grads = grads.reshape(1536, 2048)
    backprop = lax.dot_general(grads, dec, (((1,), (1,)), ((), ())), preferred_element_type=F32)
    pre_grad = jnp.where(preact > 0, backprop, 0.0)
    bias_part = jnp.zeros((4, 512), F32).at[x_hi * 2 + core].set(jnp.sum(pre_grad, axis=0))
    bias_grad = lax.psum(bias_part, "dp").reshape(2, 2, 8, 64).transpose(0, 2, 1, 3).reshape(2048)
    pre_narrow = pre_grad.astype(BF16)
    dec_prod = lax.dot_general(active, grads, (((0,), (0,)), ((), ())), preferred_element_type=F32).astype(BF16)
    enc_prod = lax.dot_general(feats, pre_narrow, (((0,), (0,)), ((), ())), preferred_element_type=F32).astype(BF16)
    dec_grad, enc_grad = pl.pallas_call(
        scatter_kernel,
        out_shape=(shape(64, 2048, dtype=F32), shape(2, 2, 32, 512, dtype=F32)),
        in_specs=[VM] * 2,
        out_specs=(VM,) * 2,
        scratch_shapes=[
            pltpu.VMEM((2, 32, 2048), BF16), pltpu.VMEM((2, 3, 64, 2048), BF16),
            pltpu.VMEM((2, 2, 32, 512), BF16), pltpu.VMEM((2, 3, 2, 2, 32, 512), BF16),
            dmas(2, 2, 4), dmas(2, 2, 4), pltpu.VMEM((2, 2, 32, 512), F32), dmas(2, 3), dmas(1),
        ],
        compiler_params=params(3),
    )(dec_prod.reshape(8, 64, 2048), enc_prod.reshape(2, 8, 2, 32, 512))
    enc_grad = enc_grad.reshape(2, 2, 32, 8, 64).transpose(2, 0, 3, 1, 4).reshape(32, 2048)
    return mean_error, enc_grad, bias_grad, dec_grad.reshape(64, 2, 1024)


def solution(mesh):
    placed = (
        P("dp", "loop"),
        P("dp", None, None),
        P("dp"),
        P("dp", "loop"),
        P("loop"),
        P(("loop", "dp"), None, None),
    )
    return jax.shard_map(
        shards,
        mesh=mesh,
        in_specs=placed,
        out_specs=(P(), P("dp", "loop"), P("loop"), P(("loop", "dp"), None, None)),
        check_vma=False,
    )
```

time: 620 us -> 346 us (0.56)
  waiting for transfers between devices: 437 us -> 0 us
  Pallas kernels: 0 us -> 162 us
  blocking collectives: 99 us -> 142 us
  between operations: 16.3 us -> 3.26 us
  local copies, waits for them, and re-layouts: 24.8 us -> 12.8 us
  matrix products: 34.8 us -> 24.1 us
    pallas_call x0 -> x3, Pallas kernels: none -> 162 us  [the longest x1 72.4 us: shards(): pl.pallas_call(lambda *refs: exchange_kernel(2.0 / math.sqrt(total_rows),...]
    all_gather x2 -> x0, waiting for transfers between devices: 162 us -> none  [the longest x1 95.9 us: shards(): decoder = lax.all_gather(dec_weight, 'dp', axis=0, tiled=True)]
    reduce_scatter x1 -> x0, waiting for transfers between devices: 155 us -> none  [shards(): lax.psum_scatter(product.reshape(lax.axis_size('dp') * dec_weight.shape[0...]
    psum x1 -> x0, waiting for transfers between devices: 75.8 us -> none  [shards(): lax.psum(partial_value.astype(jnp.bfloat16), 'loop').astype(jnp.float32)]
    psum x1 -> x2, blocking collectives: 72.6 us -> 142 us  [the longest x1 75.9 us: shards(): mean_error = lax.psum(jnp.sum(sq), ('loop', 'dp')) / (total_rows * 2048)]
    unnamed x6 -> x0, waiting for transfers between devices: 45.4 us -> none
    all_gather x1 -> x0, blocking collectives: 26.4 us -> none  [shards(): features_all = lax.all_gather(residual, 'loop', axis=1, tiled=True)]
    all_gather x1 -> x0, local copies, waits for them, and re-layouts: 11.7 us -> none  [shards(): decoder = lax.all_gather(dec_weight, 'dp', axis=0, tiled=True)]
  transfers between devices with their start and end apart: 5 -> 0, of which waited for: 5 -> 0; matrix products, arithmetic and copies ran while one was open for 3% -> 0% of each run, Pallas kernels for 0% -> 0%
where the time goes in v1:
time: 346 us
  Pallas kernels  162 us (47%)
  blocking collectives  142 us (41%)
  matrix products  24.1 us (7%)
  local copies, waits for them, and re-layouts  12.8 us (4%)
    psum x1, blocking collectives, shards(): mean_error = lax.psum(jnp.sum(sq), ('loop', 'dp')) / (total_rows * 2048)  75.9 us
    pallas_call x1, Pallas kernels, shards(): pl.pallas_call(lambda *refs: exchange_kernel(2.0 / math.sqrt(total_rows),...  72.4 us
    psum x1, blocking collectives, shards(): lax.psum(bias_part, 'dp').reshape(2, 2, 8, 64).transpose(0, 2, 1, 3)  65.9 us
    pallas_call x1, Pallas kernels, shards(): pl.pallas_call(gather_kernel, out_shape=(shape(2, 2, 384, 1024), shape(2,...  48.1 us
    pallas_call x1, Pallas kernels, shards(): pl.pallas_call(scatter_kernel, out_shape=(shape(64, 2048, dtype=F32), sha...  41.6 us
    dot_general x1, matrix products, shards(): lax.dot_general(grads, dec, (((1,), (1,)), ((), ())), preferred_element_t...  7.17 us

profile of v1, /device:TPU:1, one launch (start us, length us, event | category | flops | bytes accessed | tf_op | source)
XLA Modules:
  0.0 346.0 jit_solution(17383908881876763840)
XLA Ops:
  0.6 0.0 copy-start
  0.7 0.9 reshape.111
  1.6 0.1 reshape.112
  1.7 1.2 reshape.106
  2.9 0.9 reshape.107.enc
  3.8 1.7 copy.18
  5.5 48.1 %shard_map.93 = (bf16[2,2,384,1024]{3,2,1,0:T(8,128)(2,1)}, bf16[2,8,2,32,512]{4,3,2,1,0:T(8,128)(2,1)}, bf16[8,64,2048]{2,1,0:T(8,128)(2,1)}) custom-call(bf16[384,128]{1,0:T(8,128)(2,1)} %res.1, bf16[2,2,32,512]{3,2,1,0:T(8,128)(2,1)} %reshape.107.enc, bf16[64,2048]{1,0:T(8,128)(2,1)} %bitcast.41), custom_call_target="tpu_custom_call" | custom-call | tf_op jit(solution)/shard_map/pallas_call | solution.py:312
  53.6 4.2 %convolution_add_fusion = f32[1536,512]{1,0:T(8,128)S(1)} fusion(bf16[1536,1024]{1,0:T(8,128)(2,1)} %bitcast.51, bf16[1024,512]{1,0:T(8,128)(2,1)} %bitcast.55, f32[512]{0:T(512)S(1)} %bitcast.48), kind=kOutput, calls=%fused_computation.2 | convolution fusion | flops 1611399168 | bytes 7342080 | tf_op jit(solution)/shard_map/dot_general | solution.py:326
  57.8 5.3 %convolution_convert_fusion = bf16[1536,2048]{1,0:T(8,128)(2,1)} fusion(bf16[512,2048]{1,0:T(8,128)(2,1)S(1)} %bitcast.53, f32[1536,512]{1,0:T(8,128)S(1)} %convolution_add_fusion), kind=kOutput, calls=%fused_computation | convolution fusion | flops 3225944064 | bytes 11534336 | tf_op jit(solution)/shard_map/dot_general | solution.py:328
  63.1 0.1 constant_dynamic-slice_fusion
  63.2 0.7 copy.19
  64.6 0.7 broadcast_in_dim.5.refs_2_
  65.3 72.4 %shard_map.94 = (bf16[2,4,4,48,2048]{4,3,2,1,0:T(8,128)(2,1)}, f32[1,1024]{1,0:T(1,128)}) custom-call(bf16[2,4,4,48,2048]{4,3,2,1,0:T(8,128)(2,1)} %bitcast.36, bf16[48,2048]{1,0:T(8,128)(2,1)} %bitcast.42, f32[48,128]{1,0:T(8,128)} %broadcast_in_dim.5.refs_2_), custom_call_target="tpu_custom_call" | custom-call | tf_op jit(solution)/shard_map/pallas_call | solution.py:335
  137.6 0.0 copy-done.6
  137.7 0.0 copy-start.4
  137.7 7.2 %fusion.7 = (f32[512]{0:T(512)S(1)}, bf16[1536,512]{1,0:T(8,128)(2,1)S(1)}) fusion(bf16[1536,2048]{1,0:T(8,128)(2,1)} %bitcast.49, bf16[512,2048]{1,0:T(8,128)(2,1)S(1)} %bitcast.54, f32[1536,512]{1,0:T(8,128)} %copy-done.7), kind=kOutput, calls=%fused_computation.16 | convolution fusion | flops 3224370688 | bytes 13109248 | tf_op jit(solution)/shard_map/dot_general | solution.py:352
  144.9 2.8 fusion.2
  147.7 1.2 copy-done.8
  149.0 4.7 %convolution_convert_fusion.1 = bf16[512,2048]{1,0:T(8,128)(2,1)} fusion(bf16[1536,2048]{1,0:T(8,128)(2,1)S(1)} %bitcast.50, f32[1536,512]{1,0:T(8,128)S(1)} %copy-done.8), kind=kOutput, calls=%fused_computation.4 | convolution fusion | flops 3223846912 | bytes 11534336 | tf_op jit(solution)/shard_map/dot_general | solution.py:357
  153.6 41.6 %shard_map.95 = (f32[64,2048]{1,0:T(8,128)}, f32[2,2,32,512]{3,2,1,0:T(8,128)}) custom-call(bf16[8,64,2048]{2,1,0:T(8,128)(2,1)} %bitcast.37, bf16[2,8,2,32,512]{4,3,2,1,0:T(8,128)(2,1)} %bitcast.39), custom_call_target="tpu_custom_call" | custom-call | tf_op jit(solution)/shard_map/pallas_call | solution.py:359
  195.2 1.1 reshape.119
  196.3 0.4 copy.16
  196.7 1.2 reshape.120
  197.9 2.3 reshape.124
  200.2 0.7 and_reduce_fusion
  200.9 0.6 broadcast_select_fusion
  201.6 0.1 scatter.4
  201.6 0.1 reshape.122
  201.7 0.1 reshape.123
  201.8 65.9 %psum.15 = f32[2048]{0:T(1024)} all-reduce(f32[2048]{0:T(1024)S(1)} %reshape.123), channel_id=1, replica_groups=mesh['loop'=8,'dp'=32] {'dp'}, use_global_device_ids=true, to_apply=%region_4.5 | all-reduce | flops 2048 | bytes 16384 | tf_op jit(solution)/shard_map/psum | solution.py:355
  267.7 0.6 reduce_sum.18
  268.3 75.9 %psum.14 = f32[]{:T(128)} all-reduce(f32[]{:T(128)} %reduce_sum.18), channel_id=1, replica_groups=mesh['loop'=8,'dp'=32] {'loop','dp'}, use_global_device_ids=true, to_apply=%region_1.2 | all-reduce | flops 1 | bytes 8 | tf_op jit(solution)/shard_map/psum | solution.py:350
  (20 shorter events, 0.1 us)
Async XLA Ops:
  0.6 62.4 %copy-start = (bf16[384,2,1024]{2,1,0:T(2,128)(2,1)S(1)}, bf16[384,2,1024]{2,1,0:T(2,128)(2,1)}, u32[]{:S(2)}) copy-start(bf16[384,2,1024]{2,1,0:T(2,128)(2,1)} %param.9) | copy-start | bytes 4718596
  53.6 4.2 %copy-start.5 = (bf16[8,64,2048]{2,1,0:T(8,128)(2,1)S(1)}, bf16[8,64,2048]{2,1,0:T(8,128)(2,1)}, u32[]{:S(2)}) copy-start(bf16[8,64,2048]{2,1,0:T(8,128)(2,1)} %get-tuple-element.25) | copy-start | bytes 6291460
  57.8 5.3 %copy-start.7 = (f32[1536,512]{1,0:T(8,128)}, f32[1536,512]{1,0:T(8,128)S(1)}, u32[]{:S(2)}) copy-start(f32[1536,512]{1,0:T(8,128)S(1)} %convolution_add_fusion) | copy-start | bytes 9437188
  65.3 72.4 %copy-start.6 = (bf16[8,64,2048]{2,1,0:T(8,128)(2,1)S(1)}, bf16[8,64,2048]{2,1,0:T(8,128)(2,1)}, u32[]{:S(2)}) copy-start(bf16[8,64,2048]{2,1,0:T(8,128)(2,1)} %get-tuple-element.25) | copy-start | bytes 6291460
  137.7 7.2 %copy-start.4 = (bf16[2,2,384,1024]{3,2,1,0:T(8,128)(2,1)S(1)}, bf16[2,2,384,1024]{3,2,1,0:T(8,128)(2,1)}, u32[]{:S(2)}) copy-start(bf16[2,2,384,1024]{3,2,1,0:T(8,128)(2,1)} %get-tuple-element.23) | copy-start | bytes 9437188
  144.9 2.9 copy-start.3
  144.9 4.1 %copy-start.8 = (f32[1536,512]{1,0:T(8,128)S(1)}, f32[1536,512]{1,0:T(8,128)}, u32[]{:S(2)}) copy-start(f32[1536,512]{1,0:T(8,128)} %copy-done.7) | copy-start | bytes 9437188
  153.6 46.6 %copy-start.2 = (s32[2]{0:T(128)S(1)}, s32[2]{0:T(128)}, u32[]{:S(2)}) copy-start(s32[2]{0:T(128)} %constant.73.clone.1) | copy-start | bytes 28
  153.6 114.1 %copy-start.1 = (f32[1,1024]{1,0:T(1,128)S(1)}, f32[1,1024]{1,0:T(1,128)}, u32[]{:S(2)}) copy-start(f32[1,1024]{1,0:T(1,128)} %get-tuple-element.26) | copy-start | bytes 12292

commit v2 on v1

v2 whole, which is shorter than its diff:
```python
import math

import jax
import jax.numpy as jnp
from jax import lax
from jax.experimental import pallas as pl
from jax.experimental.pallas import tpu as pltpu
from jax.sharding import PartitionSpec as P

MESH = pl.DeviceIdType.MESH
BF16 = jnp.bfloat16
F32 = jnp.float32


def place():
    loop, dp = lax.axis_index("loop"), lax.axis_index("dp")
    x = (dp // 16) * 2 + loop // 4
    return x, loop % 4, (dp % 16) // 2, dp % 2


def ident(x, y, z, core):
    return ((x % 2) * 4 + y, (x // 2) * 16 + z * 2 + core)


def greet(peers):
    barrier = pltpu.get_barrier_semaphore()
    for peer in peers:
        pl.semaphore_signal(barrier, inc=1, device_id=peer, device_id_type=MESH)
    pl.semaphore_wait(barrier, len(peers))


def remote(src, dst, send, recv, peer):
    return pltpu.make_async_remote_copy(
        src_ref=src, dst_ref=dst, send_sem=send, recv_sem=recv, device_id=peer, device_id_type=MESH
    )


class Gather:
    def __init__(self, n, at, right, left, whole, half, sems):
        self.n, self.at, self.right, self.left = n, at, right, left
        self.whole, self.half, self.sems = whole, half, sems
        self.steps = []

    def step(self):
        s = len(self.steps)
        if s:
            for copy in self.steps[-1]:
                copy.wait_recv()
        if s == self.n // 2:
            return
        pair = []
        for side, peer in ((0, self.right), (1, self.left)):
            block = (self.at + (self.n - s if side == 0 else s)) % self.n
            last = s == self.n // 2 - 1
            if last and self.half is None and side == 1:
                continue
            ref = self.half(block, side) if last and self.half is not None else self.whole(block)
            copy = remote(ref, ref, self.sems.at[0, side, s], self.sems.at[1, side, s], peer)
            copy.start()
            pair.append(copy)
        self.steps.append(pair)

    def drain(self):
        for pair in self.steps:
            for copy in pair:
                copy.wait_send()


def add_into(ref, other):
    ref[...] = (ref[...].astype(F32) + other[...].astype(F32)).astype(BF16)


class Reduce:
    def __init__(self, n, at, right, left, whole, half, landed, sems):
        self.n, self.at, self.right, self.left = n, at, right, left
        self.whole, self.half, self.landed, self.sems = whole, half, landed, sems
        self.steps = []

    def step(self):
        s = len(self.steps)
        depth = self.n // 2
        pair = []
        for side, peer in ((0, self.right), (1, self.left)):
            if s:
                self.steps[-1][side].wait_recv()
            if s == depth:
                continue
            far = depth - s
            block = (self.at + (far if side == 0 else self.n - far)) % self.n
            if s:
                part = self.half(block, side) if s == 1 else self.whole(block)
                add_into(part, self.landed[side][s - 1])
            ref = self.half(block, side) if s == 0 else self.whole(block)
            copy = remote(ref, self.landed[side][s], self.sems.at[0, side, s], self.sems.at[1, side, s], peer)
            copy.start()
            pair.append(copy)
        if s < depth:
            self.steps.append(pair)

    def drain(self):
        for pair in self.steps:
            for copy in pair:
                copy.wait_send()


def dot(a, b, dims=((1,), (0,))):
    return lax.dot_general(a, b, (dims, ((), ())), preferred_element_type=F32)


def step_kernel(
    scale, res, enc, dec, bias, goal, valid, dec_out, enc_out, bias_out, sq_out,
    res_all, enc_all, dec_all, pre, active, act_t, res_t, sent, crossed, mine, grads,
    a1, a2, b1, b2, c1, c2, d1, d2, mid_a, mid_b, back, narrow, dec_prod, enc_prod,
    dr1, drn, er1, ern, esum, squares, sq_y, sq_x, sq_c, small, small_sum,
    ysem, xsem, esem, dsem, qsem, csem, lsem, psem, bsem, osem, sysem, sxsem, scsem,
    dsem2, esem2, msem, q2sem, q3sem,
):
    x, y, z, core = place()
    x_hi = x // 2
    up, down = ident(x, y, (z + 1) % 8, core), ident(x, y, (z + 7) % 8, core)
    east, west = ident((x + 1) % 4, y, z, core), ident((x + 3) % 4, y, z, core)
    north, south = ident(x, (y + 1) % 4, z, core), ident(x, (y + 3) % 4, z, core)
    other = ident(x, y, z, 1 - core)
    quad = [(1 - x_hi, core), (x_hi, 1 - core), (1 - x_hi, 1 - core)]
    quad_ids = [ident((x + 2) % 4, y, z, core), other, ident((x + 2) % 4, y, z, 1 - core)]
    greet([up, down, east, west, north, south] + quad_ids)
    drains = []

    def cols(block, width):
        return pl.ds(pl.multiple_of(block * width, width), width)

    def feature(xx, yy):
        return res_all.at[core, xx // 2, :, cols((xx % 2) * 4 + yy, 128)]

    local = [
        pltpu.make_async_copy(res, feature(x, y), lsem.at[0]),
        pltpu.make_async_copy(enc.at[x_hi, core], enc_all.at[x_hi, z, core], lsem.at[1]),
        pltpu.make_async_copy(dec, dec_all.at[:, z], lsem.at[2]),
    ]
    for copy in local:
        copy.start()
    swap = []
    for i, (q, peer) in enumerate(zip(quad, quad_ids)):
        copy = remote(enc.at[q[0], q[1]], enc_all.at[x_hi, z, core], qsem.at[0, i], qsem.at[1, i], peer)
        copy.start()
        swap.append(copy)
    for copy in local:
        copy.wait()
    ring_y = Gather(
        4, y, north, south, lambda b: feature(x, b),
        lambda b, h: res_all.at[core, x_hi, pl.ds(192 * h, 192), cols((x % 2) * 4 + b, 128)], ysem,
    )
    ring_x = Gather(
        4, x, east, west, lambda b: res_all.at[core, b // 2, :, cols(b % 2, 512)],
        lambda b, h: res_all.at[core, b // 2, pl.ds(192 * h, 192), cols(b % 2, 512)], xsem,
    )
    ring_e = Gather(8, z, up, down, lambda b: enc_all.at[:, b], lambda b, h: enc_all.at[h, b], esem)
    ring_d = [
        Gather(
            8, z, up, down, lambda b, t=t: dec_all.at[t, b],
            lambda b, h, t=t: dec_all.at[t, b, pl.ds(32 * h, 32)], dsem.at[t],
        )
        for t in range(2)
    ]
    drains += [ring_y, ring_x, ring_e] + ring_d
    ring_y.step()
    for copy in swap:
        copy.wait_recv()
    ring_e.step()
    ring_d[0].step()
    ring_y.step()
    ring_y.step()
    ring_x.step()
    ring_e.step()
    ring_d[0].step()
    ring_x.step()
    ring_e.step()
    ring_d[0].step()
    ring_e.step()
    ring_d[1].step()
    ring_x.step()
    cross = remote(res_all.at[core], res_all.at[core], csem.at[0], csem.at[1], other)
    cross.start()
    ring_d[0].step()
    ring_e.step()
    ring_d[1].step()
    cross.wait_recv()

    def encode(i, _):
        rows = pl.ds(pl.multiple_of(384 * i, 384), 384)
        value = dot(res_all[i // 2, i % 2], enc_all[...].reshape(1024, 512)) + bias[...]
        pre[rows, :] = value
        active[rows, :] = jnp.maximum(value, 0.0).astype(BF16)
        return 0

    lax.fori_loop(0, 4, encode, 0)
    ring_d[0].step()

    def latent_rows(c, i):
        return pl.ds(pl.multiple_of(768 * c + 192 * i, 192), 192)

    def decode(t, c, i):
        return dot(active[latent_rows(c, i), :], dec_all[t].reshape(512, 1024)).reshape(4, 48, 1024)

    def hand(t, i):
        return remote(sent.at[t, i], crossed.at[t, i], psem.at[t, 0, i], psem.at[t, 1, i], other)

    def decode_other(t):
        def one(i, _):
            sent[t, i] = decode(t, 1 - core, i).astype(BF16)
            hand(t, i).start()
            return 0

        lax.fori_loop(0, 4, one, 0)

    def decode_mine(t):
        def one(i, _):
            value = decode(t, core, i)
            hand(t, i).wait_recv()
            mine[t, i] = (value + crossed[t, i].astype(F32)).astype(BF16)
            return 0

        lax.fori_loop(0, 4, one, 0)

    lo, hi = pl.ds(0, 512), pl.ds(512, 512)
    ok = valid[:, 0:1]

    def exchange(t):
        own, out = mine.at[t], grads.at[t, core]
        red_a = Reduce(
            4, x, east, west, lambda b: own.at[b, :, :, lo], lambda b, h: own.at[b, pl.ds(2 * h, 2), :, lo],
            [[a1.at[t, s], a2.at[t, s]] for s in range(2)], bsem.at[t, 0],
        )
        red_b = Reduce(
            4, y, north, south, lambda b: own.at[:, b, :, hi], lambda b, h: own.at[pl.ds(2 * h, 2), b, :, hi],
            [[b1.at[t, s], b2.at[t, s]] for s in range(2)], bsem.at[t, 1],
        )
        red_c = Reduce(
            4, y, north, south, lambda b: mid_a.at[t, b], lambda b, h: mid_a.at[t, b, :, pl.ds(256 * h, 256)],
            [[c1.at[t, s], c2.at[t, s]] for s in range(2)], bsem.at[t, 2],
        )
        red_d = Reduce(
            4, x, east, west, lambda b: mid_b.at[t, b], lambda b, h: mid_b.at[t, b, :, pl.ds(256 * h, 256)],
            [[d1.at[t, s], d2.at[t, s]] for s in range(2)], bsem.at[t, 3],
        )
        ring_c = Gather(
            4, y, north, south, lambda b: out.at[x, b, :, lo],
            lambda b, h: out.at[x, b, :, pl.ds(256 * h, 256)], bsem.at[t, 4],
        )
        ring_d = Gather(
            4, x, east, west, lambda b: out.at[b, y, :, hi],
            lambda b, h: out.at[b, y, :, pl.ds(512 + 256 * h, 256)], bsem.at[t, 5],
        )
        ring_a = Gather(
            4, x, east, west, lambda b: out.at[b, :, :, lo], lambda b, h: out.at[b, pl.ds(2 * h, 2), :, lo],
            bsem.at[t, 6],
        )
        ring_b = Gather(
            4, y, north, south, lambda b: out.at[:, b, :, hi], lambda b, h: out.at[pl.ds(2 * h, 2), b, :, hi],
            bsem.at[t, 7],
        )
        sum_y = Gather(4, y, north, south, lambda b: sq_y.at[b], None, sysem)
        sum_x = Gather(4, x, east, west, lambda b: sq_x.at[b], None, sxsem)
        sum_c = remote(sq_c.at[core], sq_c.at[core], scsem.at[0], scsem.at[1], other)
        cross = [remote(out.at[:, :, :, w], out.at[:, :, :, w], osem.at[t, i, 0], osem.at[t, i, 1], other)
                 for i, w in enumerate((lo, hi))]
        drains.extend([red_a, red_b, red_c, red_d, ring_a, ring_b, ring_c, ring_d])
        if t == 1:
            drains.extend([sum_y, sum_x])

        def misfit(where, landed, middle, at):
            rebuilt = middle[t, at].astype(F32) + landed[t, 0].astype(F32) + landed[t, 1].astype(F32)
            miss = (rebuilt - goal[t, :, where].astype(F32)) * ok
            out[x, y, :, where] = (scale * miss).astype(BF16)
            square = miss * miss
            parts = [square[8 * i : 8 * i + 8, 128 * j : 128 * j + 128] for i in range(6) for j in range(4)]
            squares[...] += sum(parts[1:], parts[0])

        red_a.step()
        red_b.step()
        yield
        red_a.step()
        red_b.step()
        yield
        red_a.step()
        mid_a[t] = (own[x, :, :, lo].astype(F32) + a2[t, 0].astype(F32) + a2[t, 1].astype(F32)).astype(BF16)
        red_c.step()
        red_b.step()
        mid_b[t] = (own[:, y, :, hi].astype(F32) + b2[t, 0].astype(F32) + b2[t, 1].astype(F32)).astype(BF16)
        red_d.step()
        yield
        red_c.step()
        red_d.step()
        yield
        red_c.step()
        misfit(lo, c2, mid_a, y)
        ring_c.step()
        red_d.step()
        misfit(hi, d2, mid_b, x)
        ring_d.step()
        if t == 1:
            sq_y[y] = squares[...]
            sum_y.step()
        yield
        ring_c.step()
        ring_d.step()
        if t == 1:
            sum_y.step()
        yield
        ring_c.step()
        ring_a.step()
        ring_d.step()
        ring_b.step()
        if t == 1:
            sum_y.step()
            sq_x[x] = (sq_y[0] + sq_y[1]) + (sq_y[2] + sq_y[3])
            sum_x.step()
        yield
        ring_a.step()
        ring_b.step()
        if t == 1:
            sum_x.step()
        yield
        ring_a.step()
        cross[0].start()
        ring_b.step()
        cross[1].start()
        if t == 1:
            sum_x.step()
            sq_c[core] = (sq_x[0] + sq_x[1]) + (sq_x[2] + sq_x[3])
            sum_c.start()
        yield
        cross[0].wait()
        cross[1].wait()
        if t == 1:
            sum_c.wait()
            small[z, :, 512:640] = sq_c[0] + sq_c[1]

    squares[...] = jnp.zeros_like(squares)
    first, second = exchange(0), exchange(1)

    def flip_features(i, _):
        res_t[:, cols(i, 384)] = res_all[i // 2, i % 2].T
        return 0

    def flip_latents(i, _):
        act_t[:, cols(i, 384)] = active[pl.ds(pl.multiple_of(384 * i, 384), 384), :].T
        return 0

    decode_other(0)
    decode_mine(0)
    next(first)
    ring_d[1].step()
    next(first)
    ring_d[1].step()
    next(first)
    lax.fori_loop(0, 4, flip_latents, 0)
    ring_d[1].step()
    decode_other(1)
    next(first)
    decode_mine(1)
    next(second)
    next(first)
    next(second)
    next(first)
    lax.fori_loop(0, 4, flip_features, 0)
    next(second)
    next(first)
    next(second)
    next(first)
    next(second)
    next(first)
    next(second)
    next(first, None)

    def decoder_product(t):
        def one(i, _):
            value = dot(act_t[...], grads[t, :, :, :, :, cols(i, 256)].reshape(1536, 256))
            dec_prod[t, :, :, cols(i, 256)] = value.astype(BF16).reshape(8, 64, 256)
            return 0

        lax.fori_loop(0, 4, one, 0)

    red_d = [
        Reduce(
            8, z, up, down, lambda b, t=t: dec_prod.at[t, b], lambda b, h, t=t: dec_prod.at[t, b, pl.ds(32 * h, 32)],
            [[dr1.at[t, s]] + [drn.at[t, s, i] for i in range(3)] for s in range(2)], dsem2.at[t],
        )
        for t in range(2)
    ]
    red_e = Reduce(
        8, z, up, down, lambda b: enc_prod.at[:, b], lambda b, h: enc_prod.at[h, b],
        [[er1.at[s]] + [ern.at[s, i] for i in range(3)] for s in range(2)], esem2,
    )
    ring_m = Gather(8, z, up, down, lambda b: small.at[b], None, msem)
    drains += red_d + [red_e, ring_m]
    next(second)
    decoder_product(0)
    red_d[0].step()

    def spread(t, c, i):
        return dot(grads[t, c, i].reshape(192, 1024), dec_all[t].reshape(512, 1024), ((1,), (1,)))

    def spread_first(i, _):
        back[latent_rows(i // 4, i % 4), :] = spread(0, i // 4, i % 4)
        return 0

    next(second)
    lax.fori_loop(0, 8, spread_first, 0)
    red_d[0].step()
    next(second)
    next(second, None)
    red_d[0].step()

    def spread_second(i, total):
        rows = latent_rows(i // 4, i % 4)
        value = back[rows, :] + spread(1, i // 4, i % 4)
        value = jnp.where(pre[rows, :] > 0, value, 0.0)
        narrow[rows, :] = value.astype(BF16)
        return total + jnp.sum(value.reshape(24, 8, 512), axis=0)

    total = lax.fori_loop(0, 8, spread_second, jnp.zeros((8, 512), F32))
    small[z, :, 0:512] = total
    ring_m.step()
    red_d[0].step()

    def encoder_product(i, _):
        rows = pl.ds(pl.multiple_of(256 * i, 256), 256)
        value = dot(res_t[rows, :], narrow[...])
        for j in range(4):
            enc_prod[i // 2, (i % 2) * 4 + j] = value[64 * j : 64 * j + 64].astype(BF16).reshape(2, 32, 512)
        return 0

    lax.fori_loop(0, 4, encoder_product, 0)
    red_e.step()
    decoder_product(1)
    red_d[1].step()
    red_d[0].step()
    ring_m.step()
    red_e.step()
    red_d[1].step()
    ring_m.step()
    red_e.step()
    red_d[1].step()
    ring_m.step()
    red_e.step()
    red_d[1].step()
    dec_out[0] = dec_prod[0, z].astype(F32) + drn[0, 0, 2].astype(F32) + drn[0, 1, 2].astype(F32)
    red_e.step()
    esum[...] = enc_prod[:, z].astype(F32) + ern[0, 2].astype(F32) + ern[1, 2].astype(F32)
    keep = [pltpu.make_async_copy(esum.at[x_hi, core], enc_out.at[x_hi, core], lsem.at[3])]
    keep[0].start()
    for i, (q, peer) in enumerate(zip(quad, quad_ids)):
        copy = remote(esum.at[q[0], q[1]], enc_out.at[x_hi, core], q2sem.at[0, i], q2sem.at[1, i], peer)
        copy.start()
        keep.append(copy)
    ring_m.step()
    full = ((small[0] + small[1]) + (small[2] + small[3])) + ((small[4] + small[5]) + (small[6] + small[7]))
    sq_out[...] = full[:, 512:640]
    small_sum[...] = full[:, 0:512]
    keep.append(pltpu.make_async_copy(small_sum, bias_out.at[x_hi, core], lsem.at[4]))
    keep[-1].start()
    for i, peer in enumerate(quad_ids):
        copy = remote(small_sum, bias_out.at[x_hi, core], q3sem.at[0, i], q3sem.at[1, i], peer)
        copy.start()
        keep.append(copy)
    red_d[1].step()
    dec_out[1] = dec_prod[1, z].astype(F32) + drn[1, 0, 2].astype(F32) + drn[1, 1, 2].astype(F32)
    for copy in keep:
        copy.wait()
    for copy in swap:
        copy.wait_send()
    cross.wait_send()
    for t in range(2):
        for i in range(4):
            hand(t, i).wait_send()
    for ring in drains:
        ring.drain()


VM = pl.BlockSpec(memory_space=pltpu.VMEM)


def dmas(*shape):
    return pltpu.SemaphoreType.DMA(shape)


def params(ident):
    return pltpu.CompilerParams(collective_id=ident, has_side_effects=True, vmem_limit_bytes=56 << 20)


def shape(*dims, dtype=BF16):
    return jax.ShapeDtypeStruct(dims, dtype)


def shards(residual, targets, counts, enc_weight, enc_bias, dec_weight):
    loop, dp = lax.axis_index("loop"), lax.axis_index("dp")
    x_hi, core = dp // 16, dp % 2
    enc_quad = enc_weight.reshape(32, 2, 8, 2, 64).transpose(1, 3, 0, 2, 4).reshape(2, 2, 32, 512)
    bias = lax.dynamic_index_in_dim(
        enc_bias.reshape(2, 8, 2, 64).transpose(0, 2, 1, 3).reshape(4, 512), x_hi * 2 + core, 0, True
    )
    goal = lax.dynamic_slice_in_dim(targets, loop * 48, 48, 0).transpose(1, 0, 2)
    rows = loop * 48 + lax.iota(jnp.int32, 48)
    valid = jnp.broadcast_to((rows < counts[0]).astype(F32)[:, None], (48, 128))
    total_rows = 32 * 384 // 2
    vm = pltpu.VMEM
    dec_grad, enc_grad, bias_grad, sq = pl.pallas_call(
        lambda *refs: step_kernel(2.0 / math.sqrt(total_rows), *refs),
        out_shape=(
            shape(2, 64, 1024, dtype=F32), shape(2, 2, 32, 512, dtype=F32),
            shape(2, 2, 8, 512, dtype=F32), shape(8, 128, dtype=F32),
        ),
        in_specs=[VM] * 6,
        out_specs=(VM,) * 4,
        scratch_shapes=[
            vm((2, 2, 384, 1024), BF16), vm((2, 8, 2, 32, 512), BF16), vm((2, 8, 64, 1024), BF16),
            vm((1536, 512), F32), vm((1536, 512), BF16), vm((512, 1536), BF16), vm((1024, 1536), BF16),
            vm((2, 4, 4, 48, 1024), BF16), vm((2, 4, 4, 48, 1024), BF16), vm((2, 4, 4, 48, 1024), BF16),
            vm((2, 2, 4, 4, 48, 1024), BF16),
            vm((2, 2, 2, 48, 512), BF16), vm((2, 2, 4, 48, 512), BF16),
            vm((2, 2, 2, 48, 512), BF16), vm((2, 2, 4, 48, 512), BF16),
            vm((2, 2, 48, 256), BF16), vm((2, 2, 48, 512), BF16),
            vm((2, 2, 48, 256), BF16), vm((2, 2, 48, 512), BF16),
            vm((2, 4, 48, 512), BF16), vm((2, 4, 48, 512), BF16),
            vm((1536, 512), F32), vm((1536, 512), BF16),
            vm((2, 8, 64, 1024), BF16), vm((2, 8, 2, 32, 512), BF16),
            vm((2, 2, 32, 1024), BF16), vm((2, 2, 3, 64, 1024), BF16),
            vm((2, 2, 32, 512), BF16), vm((2, 3, 2, 2, 32, 512), BF16), vm((2, 2, 32, 512), F32),
            vm((8, 128), F32), vm((4, 8, 128), F32), vm((4, 8, 128), F32), vm((2, 8, 128), F32),
            vm((8, 8, 640), F32), vm((8, 512), F32),
            dmas(2, 2, 2), dmas(2, 2, 2), dmas(2, 2, 4), dmas(2, 2, 2, 4), dmas(2, 3), dmas(2), dmas(5),
            dmas(2, 2, 4), dmas(2, 8, 2, 2, 2), dmas(2, 2, 2), dmas(2, 2, 2), dmas(2, 2, 2), dmas(2),
            dmas(2, 2, 2, 4), dmas(2, 2, 4), dmas(2, 2, 4), dmas(2, 3), dmas(2, 3),
        ],
        compiler_params=params(1),
    )(residual, enc_quad, dec_weight.transpose(1, 0, 2), bias, goal, valid)
    mean_error = jnp.sum(sq) / (total_rows * 2048)
    enc_grad = enc_grad.reshape(2, 2, 32, 8, 64).transpose(2, 0, 3, 1, 4).reshape(32, 2048)
    bias_grad = jnp.sum(bias_grad, axis=2).reshape(2, 2, 8, 64).transpose(0, 2, 1, 3).reshape(2048)
    return mean_error, enc_grad, bias_grad, dec_grad.transpose(1, 0, 2)


def solution(mesh):
    placed = (
        P("dp", "loop"),
        P("dp", None, None),
        P("dp"),
        P("dp", "loop"),
        P("loop"),
        P(("loop", "dp"), None, None),
    )
    return jax.shard_map(
        shards,
        mesh=mesh,
        in_specs=placed,
        out_specs=(P(), P("dp", "loop"), P("loop"), P(("loop", "dp"), None, None)),
        check_vma=False,
    )
```

time: 346 us -> 160 us (0.46)
  blocking collectives: 142 us -> 0 us
  matrix products: 24.1 us -> 0 us
  Pallas kernels: 162 us -> 144 us
    psum x2 -> x0, blocking collectives: 142 us -> none  [the longest x1 75.9 us: shards(): mean_error = lax.psum(jnp.sum(sq), ('loop', 'dp')) / (total_rows * 2048)]
    dot_general x5 -> x0, matrix products: 24.1 us -> none  [the longest x1 7.17 us: shards(): lax.dot_general(grads, dec, (((1,), (1,)), ((), ())), preferred_element_t...]
    pallas_call x3 -> x1, Pallas kernels: 162 us -> 144 us  [shards(): pl.pallas_call(lambda *refs: step_kernel(2.0 / math.sqrt(total_rows), *re...]
where the time goes in v2:
time: 160 us
  Pallas kernels  144 us (90%)
  local copies, waits for them, and re-layouts  10.5 us (7%)
  between operations  3.28 us (2%)
  other arithmetic  2.22 us (1%)
    pallas_call x1, Pallas kernels, shards(): pl.pallas_call(lambda *refs: step_kernel(2.0 / math.sqrt(total_rows), *re...  144 us

profile of v2, /device:TPU:1, one launch (start us, length us, event | category | flops | bytes accessed | tf_op | source)
XLA Modules:
  0.0 160.0 jit_solution(16018899888665042155)
XLA Ops:
  0.6 0.0 copy-start
  0.6 0.0 copy-start.2
  1.5 0.8 reshape.40
  2.3 0.1 reshape.41
  2.3 0.6 constant_dynamic-slice_fusion.1.refs_3_
  2.9 0.7 broadcast_in_dim.2.refs_5_
  3.6 0.0 copy-done
  3.6 0.1 constant_dynamic-slice_fusion
  3.7 0.7 copy.34
  4.5 1.2 reshape.38
  5.7 0.9 reshape.39.refs_1_
  6.5 0.0 copy-done.2
  6.5 0.8 copy.32
  7.3 144.1 %shard_map.93 = (f32[2,64,1024]{2,1,0:T(8,128)}, f32[2,2,32,512]{3,2,1,0:T(8,128)}, f32[2,2,8,512]{3,2,1,0:T(8,128)}, f32[8,128]{1,0:T(8,128)}) custom-call(bf16[384,128]{1,0:T(8,128)(2,1)} %refs_0_.1, bf16[2,2,32,512]{3,2,1,0:T(8,128)(2,1)} %reshape.39.refs_1_, bf16[2,64,1024]{2,1,0:T(8,128)(2,1)} %bitcast.23, ...), custom_call_target="tpu_custom_call" | custom-call | tf_op jit(solution)/shard_map/pallas_call | solution.py:508
  151.4 0.0 copy-start.1
  151.4 1.3 reduce_sum.18
  153.4 0.9 reduce_sum.19
  154.2 0.1 reshape.44
  154.3 0.7 reshape.45
  155.0 1.1 reshape.42
  156.1 0.4 copy.25
  156.5 1.2 reshape.43
  157.7 0.0 copy-done.1
  157.7 1.2 copy.27
  (4 shorter events, 0.1 us)
Async XLA Ops:
  0.6 3.0 %copy-start = (bf16[384,2,1024]{2,1,0:T(2,128)(2,1)S(1)}, bf16[384,2,1024]{2,1,0:T(2,128)(2,1)}, u32[]{:S(2)}) copy-start(bf16[384,2,1024]{2,1,0:T(2,128)(2,1)} %param.7) | copy-start | bytes 4718596
  0.6 5.9 %copy-start.2 = (bf16[64,2,1024]{2,1,0:T(2,128)(2,1)S(1)}, bf16[64,2,1024]{2,1,0:T(2,128)(2,1)}, u32[]{:S(2)}) copy-start(bf16[64,2,1024]{2,1,0:T(2,128)(2,1)} %param.11) | copy-start | bytes 786436
  151.4 6.3 %copy-start.1 = (f32[2,64,1024]{2,1,0:T(8,128)S(1)}, f32[2,64,1024]{2,1,0:T(8,128)}, u32[]{:S(2)}) copy-start(f32[2,64,1024]{2,1,0:T(8,128)} %get-tuple-element.11) | copy-start | bytes 1572868

commit v3 on v0

v3 whole, which is shorter than its diff:
```python
import math

import jax
import jax.numpy as jnp
from jax import lax
from jax.experimental import pallas as pl
from jax.experimental.pallas import tpu as pltpu
from jax.sharding import PartitionSpec as P

MESH = pl.DeviceIdType.MESH
BF16 = jnp.bfloat16
F32 = jnp.float32


def place():
    loop, dp = lax.axis_index("loop"), lax.axis_index("dp")
    x = (dp // 16) * 2 + loop // 4
    return x, loop % 4, (dp % 16) // 2, dp % 2


def ident(x, y, z, core):
    return ((x % 2) * 4 + y, (x // 2) * 16 + z * 2 + core)


def greet(peers):
    barrier = pltpu.get_barrier_semaphore()
    for peer in peers:
        pl.semaphore_signal(barrier, inc=1, device_id=peer, device_id_type=MESH)
    pl.semaphore_wait(barrier, len(peers))


def remote(src, dst, send, recv, peer):
    return pltpu.make_async_remote_copy(
        src_ref=src, dst_ref=dst, send_sem=send, recv_sem=recv, device_id=peer, device_id_type=MESH
    )


class Gather:
    def __init__(self, n, at, right, left, whole, half, sems):
        self.n, self.at, self.right, self.left = n, at, right, left
        self.whole, self.half, self.sems = whole, half, sems
        self.steps = []

    def step(self):
        s = len(self.steps)
        if s:
            for copy in self.steps[-1]:
                copy.wait_recv()
        if s == self.n // 2:
            return
        pair = []
        for side, peer in ((0, self.right), (1, self.left)):
            block = (self.at + (self.n - s if side == 0 else s)) % self.n
            last = s == self.n // 2 - 1
            if last and self.half is None and side == 1:
                continue
            ref = self.half(block, side) if last and self.half is not None else self.whole(block)
            copy = remote(ref, ref, self.sems.at[0, side, s], self.sems.at[1, side, s], peer)
            copy.start()
            pair.append(copy)
        self.steps.append(pair)

    def drain(self):
        for pair in self.steps:
            for copy in pair:
                copy.wait_send()


def add_into(ref, other):
    ref[...] = (ref[...].astype(F32) + other[...].astype(F32)).astype(BF16)


class Reduce:
    def __init__(self, n, at, right, left, whole, half, landed, sems):
        self.n, self.at, self.right, self.left = n, at, right, left
        self.whole, self.half, self.landed, self.sems = whole, half, landed, sems
        self.steps = []

    def step(self):
        s = len(self.steps)
        depth = self.n // 2
        pair = []
        for side, peer in ((0, self.right), (1, self.left)):
            if s:
                self.steps[-1][side].wait_recv()
            if s == depth:
                continue
            far = depth - s
            block = (self.at + (far if side == 0 else self.n - far)) % self.n
            if s:
                part = self.half(block, side) if s == 1 else self.whole(block)
                add_into(part, self.landed[side][s - 1])
            ref = self.half(block, side) if s == 0 else self.whole(block)
            copy = remote(ref, self.landed[side][s], self.sems.at[0, side, s], self.sems.at[1, side, s], peer)
            copy.start()
            pair.append(copy)
        if s < depth:
            self.steps.append(pair)

    def drain(self):
        for pair in self.steps:
            for copy in pair:
                copy.wait_send()


GROUPS = 4
ORDER = (
    "d31", "v1", "u1", "d01", "e1", "d21", "u2", "v2", "d02", "x1", "y1", "e2",
    "d32", "d11", "x2", "y2", "e3", "d03", "d33", "yw", "xw", "e4", "d12", "d04",
    "d22", "d34", "rw", "ew", "n0", "d13", "n1", "d0w", "o0", "f0", "d23", "d3w",
    "o3", "d14", "fl", "f3", "m0", "d24", "p000", "p010", "d1w", "o1", "m3", "p300",
    "d2w", "o2", "p310", "p001", "p011", "m1", "p100", "p110", "p301", "m2", "p210", "p200",
    "p311", "p002", "f1", "p012", "p101", "p211", "ff", "p013", "p312", "p201", "p003", "p302",
    "p111", "p212", "p014", "p102", "p313", "p004", "f2", "p303", "p202", "p213", "p015", "p314",
    "p103", "p005", "p112", "p203", "p304", "p016", "p315", "p214", "p113", "p006", "p305", "p204",
    "p104", "p316", "p114", "p215", "p306", "p205", "p017", "s1", "p105", "p007", "p115", "p216",
    "p206", "p317", "p307", "p018", "p008", "p116", "s2", "p106", "p217", "p019", "p207", "p009",
    "p318", "D0", "r01", "s3", "p308", "p107", "p319", "p117", "p218", "s4", "r02", "p309",
    "p208", "D3", "p108", "r31", "p118", "p209", "p219", "D2", "r21", "p109", "r03", "p119",
    "r32", "s5", "A", "s6", "r22", "r33", "B", "b1", "r23", "r04", "E0", "b2",
    "q01", "r24", "E1", "b3", "q11", "q02", "D1", "r11", "b4", "r2w", "q12", "q03",
    "r12", "r0w", "q13", "bw", "q04", "r13", "q14", "r34", "q0w", "r14", "q1w", "r3w",
    "r1w",
)


def dot(a, b, dims=((1,), (0,))):
    return lax.dot_general(a, b, (dims, ((), ())), preferred_element_type=F32)


def step_kernel(
    groups, scale, res, enc, dec, bias, goal, valid, dec_out, enc_out, bias_out, sq_out,
    res_all, enc_all, dec_all, pre, active, act_t, res_t, dec_t, sent, crossed, mine, grads,
    far1, far2, near1, near2, mid, back, narrow, dec_prod, enc_prod,
    dr1, drn, er1, ern, esum, squares, sq_y, sq_x, sq_c, small, small_sum,
    usem, vsem, ysem, xsem, esem, dsem, qsem, csem, lsem, psem, bsem, osem, sysem, sxsem, scsem,
    dsem2, esem2, msem, q2sem, q3sem,
):
    width = 2048 // groups
    wide, thin = width // 2, width // 4
    x, y, z, core = place()
    x_hi = x // 2
    up, down = ident(x, y, (z + 1) % 8, core), ident(x, y, (z + 7) % 8, core)
    east, west = ident((x + 1) % 4, y, z, core), ident((x + 3) % 4, y, z, core)
    north, south = ident(x, (y + 1) % 4, z, core), ident(x, (y + 3) % 4, z, core)
    other = ident(x, y, z, 1 - core)
    quad = [(1 - x_hi, core), (x_hi, 1 - core), (1 - x_hi, 1 - core)]
    quad_ids = [ident((x + 2) % 4, y, z, core), other, ident((x + 2) % 4, y, z, 1 - core)]
    drains = []

    def cols(block, width):
        return pl.ds(pl.multiple_of(block * width, width), width)

    top, low = pl.ds(0, 192), pl.ds(192, 192)

    def feature(rows, xx, yy):
        return res_all.at[core, xx // 2, rows, cols((xx % 2) * 4 + yy, 128)]

    def feature_row(rows, xx):
        return res_all.at[core, xx // 2, rows, cols(xx % 2, 512)]

    def feature_both(rows, k, yy):
        return res_all.at[core, :, rows, cols(k * 4 + yy, 128)]

    local = [
        pltpu.make_async_copy(res, feature(pl.ds(0, 384), x, y), lsem.at[0]),
        pltpu.make_async_copy(enc.at[x_hi, core], enc_all.at[x_hi, z, core], lsem.at[1]),
        pltpu.make_async_copy(dec, dec_all.at[:, z], lsem.at[2]),
    ]
    for copy in local:
        copy.start()
    greet([up, down, east, west, north, south] + quad_ids)
    swap = []
    for i, (q, peer) in enumerate(zip(quad, quad_ids)):
        copy = remote(enc.at[q[0], q[1]], enc_all.at[x_hi, z, core], qsem.at[0, i], qsem.at[1, i], peer)
        copy.start()
        swap.append(copy)
    for copy in local:
        copy.wait()
    ring_e = Gather(8, z, up, down, lambda b: enc_all.at[:, b], lambda b, h: enc_all.at[h, b], esem)
    ring_d = [
        Gather(
            8, z, up, down, lambda b, t=t: dec_all.at[t, b],
            lambda b, h, t=t: dec_all.at[t, b, pl.ds(32 * h, 32)], dsem.at[t],
        )
        for t in range(groups)
    ]
    ring_u = Gather(
        4, y, north, south, lambda b: feature(top, x, b), lambda b, h: feature(pl.ds(96 * h, 96), x, b), usem
    )
    ring_v = Gather(
        4, x, east, west, lambda b: feature(low, b, y), lambda b, h: feature(pl.ds(192 + 96 * h, 96), b, y), vsem
    )
    ring_x = Gather(
        4, x, east, west, lambda b: feature_row(top, b), lambda b, h: feature_row(pl.ds(96 * h, 96), b), xsem
    )
    ring_y = [
        Gather(
            4, y, north, south, lambda b, k=k: feature_both(low, k, b),
            lambda b, h, k=k: feature_both(pl.ds(192 + 96 * h, 96), k, b), ysem.at[k],
        )
        for k in range(2)
    ]
    drains += [ring_u, ring_v, ring_x, ring_e] + ring_y + ring_d

    tasks = {"e1": lambda: ([copy.wait_recv() for copy in swap], ring_e.step())}

    def put(*names):
        def bind(action):
            for name in names:
                tasks[name] = action
            return action

        return bind

    for name in ("e2", "e3", "e4", "ew"):
        tasks[name] = ring_e.step
    for g in range(groups):
        for name in "1234w":
            tasks[f"d{g}{name}"] = ring_d[g].step
    for name in ("u1", "u2"):
        tasks[name] = ring_u.step
    for name in ("v1", "v2"):
        tasks[name] = ring_v.step
    cross = []

    def cross_over(i, rows):
        ref = res_all.at[core, :, rows]
        cross.append(remote(ref, ref, csem.at[i, 0], csem.at[i, 1], other))
        cross[-1].start()

    tasks["x1"] = lambda: (ring_u.step(), ring_x.step())
    tasks["x2"] = ring_x.step
    tasks["xw"] = lambda: (ring_x.step(), cross_over(0, top))
    tasks["y1"] = lambda: (ring_v.step(), ring_y[0].step(), ring_y[1].step())
    tasks["y2"] = lambda: (ring_y[0].step(), ring_y[1].step())
    tasks["yw"] = lambda: (ring_y[0].step(), ring_y[1].step(), cross_over(1, low))
    tasks["rw"] = lambda: [copy.wait_recv() for copy in cross]

    def encode(i, _):
        rows = pl.ds(pl.multiple_of(384 * i, 384), 384)
        value = dot(res_all[i // 2, i % 2], enc_all[...].reshape(1024, 512)) + bias[...]
        pre[rows, :] = value
        active[rows, :] = jnp.maximum(value, 0.0).astype(BF16)
        return 0

    tasks["n0"] = lambda: lax.fori_loop(0, 2, encode, 0)
    tasks["n1"] = lambda: lax.fori_loop(2, 4, encode, 0)

    def flip_features(i, _):
        res_t[:, cols(i, 384)] = res_all[i // 2, i % 2].T
        return 0

    def flip_latents(i, _):
        act_t[:, cols(i, 384)] = active[pl.ds(pl.multiple_of(384 * i, 384), 384), :].T
        return 0

    def flip_decoder(g):
        def one(i, _):
            dec_t[g, :, cols(i, 128)] = dec_all[g, pl.ds(2 * i, 2)].reshape(128, width).T
            return 0

        lax.fori_loop(0, 4, one, 0)

    tasks["ff"] = lambda: lax.fori_loop(0, 4, flip_features, 0)
    tasks["fl"] = lambda: lax.fori_loop(0, 4, flip_latents, 0)

    def latent_rows(c, i):
        return pl.ds(pl.multiple_of(768 * c + 384 * i, 384), 384)

    def decode(g, c, i):
        return dot(active[latent_rows(c, i), :], dec_all[g].reshape(512, width)).reshape(2, 4, 48, width)

    def hand(g, i):
        pair = pl.ds(2 * i, 2)
        return remote(sent.at[g, pair], crossed.at[g, pair], psem.at[g, 0, i], psem.at[g, 1, i], other)

    def decode_other(g):
        def one(i, _):
            sent[g, pl.ds(2 * i, 2)] = decode(g, 1 - core, i).astype(BF16)
            hand(g, i).start()
            return 0

        lax.fori_loop(0, 2, one, 0)

    def decode_mine(g):
        def one(i, _):
            value = decode(g, core, i)
            hand(g, i).wait_recv()
            pair = pl.ds(2 * i, 2)
            mine[g, pair] = (value + crossed[g, pair].astype(F32)).astype(BF16)
            return 0

        lax.fori_loop(0, 2, one, 0)

    ok = valid[:, 0:1]
    along_x, along_y = (4, x, east, west), (4, y, north, south)
    squares[...] = jnp.zeros_like(squares)

    def exchange(g, q):
        own, out = mine.at[g], grads.at[g, core]
        w = pl.ds(q * wide, wide)
        first, then = (along_x, along_y) if q == 0 else (along_y, along_x)
        at, near = first[1], then[1]

        def lane(ref, b):
            return ref.at[b, :, :, w] if q == 0 else ref.at[:, b, :, w]

        def half_lane(ref, b, h):
            pair = pl.ds(2 * h, 2)
            return ref.at[b, pair, :, w] if q == 0 else ref.at[pair, b, :, w]

        def cell(b, where):
            return out.at[x, b, :, where] if q == 0 else out.at[b, y, :, where]

        def part(h):
            return pl.ds(q * wide + thin * h, thin)

        sems = bsem.at[g, q]
        red_far = Reduce(
            *first, lambda b: lane(own, b), lambda b, h: half_lane(own, b, h),
            [[far1.at[g, q, s], far2.at[g, q, s]] for s in range(2)], sems.at[0],
        )
        red_near = Reduce(
            *then, lambda b: mid.at[g, q, b], lambda b, h: mid.at[g, q, b, :, pl.ds(thin * h, thin)],
            [[near1.at[g, q, s], near2.at[g, q, s]] for s in range(2)], sems.at[1],
        )
        ring_near = Gather(*then, lambda b: cell(b, w), lambda b, h: cell(b, part(h)), sems.at[2])
        ring_far = Gather(*first, lambda b: lane(out, b), lambda b, h: half_lane(out, b, h), sems.at[3])
        drains.extend([red_far, red_near, ring_near, ring_far])
        over = []

        def hand_over(k):
            ref = lane(out, (at + k) % 4)
            over.append(remote(ref, ref, osem.at[g, q, 0, k], osem.at[g, q, 1, k], other))
            over[-1].start()

        red_far.step()
        yield
        red_far.step()
        yield
        red_far.step()
        mid[g, q] = (
            lane(own, at)[...].astype(F32) + far2[g, q, 0].astype(F32) + far2[g, q, 1].astype(F32)
        ).astype(BF16)
        red_near.step()
        yield
        red_near.step()
        yield
        red_near.step()
        rebuilt = mid[g, q, near].astype(F32) + near2[g, q, 0].astype(F32) + near2[g, q, 1].astype(F32)
        miss = (rebuilt - goal[g, :, w].astype(F32)) * ok
        cell(near, w)[...] = (scale * miss).astype(BF16)
        ring_near.step()
        square = miss * miss
        parts = [
            square[8 * i : 8 * i + 8, 128 * j : 128 * j + 128] for i in range(6) for j in range(wide // 128)
        ]
        squares[...] += sum(parts[1:], parts[0])
        yield
        ring_near.step()
        yield
        ring_near.step()
        ring_far.step()
        hand_over(0)
        yield
        ring_far.step()
        hand_over(1)
        hand_over(3)
        yield
        ring_far.step()
        hand_over(2)
        yield
        for copy in over:
            copy.wait()
        yield

    def decoder_product(g):
        def one(i, _):
            value = dot(act_t[...], grads[g, :, :, :, :, cols(i, 256)].reshape(1536, 256))
            dec_prod[g, :, :, cols(i, 256)] = value.astype(BF16).reshape(8, 64, 256)
            return 0

        lax.fori_loop(0, width // 256, one, 0)

    def finish_decoder(g, ring):
        ring.step()
        dec_out[g] = dec_prod[g, z].astype(F32) + drn[g, 0, 2].astype(F32) + drn[g, 1, 2].astype(F32)

    for g in range(groups):
        tasks[f"o{g}"] = lambda g=g: decode_other(g)
        tasks[f"m{g}"] = lambda g=g: decode_mine(g)
        tasks[f"f{g}"] = lambda g=g: flip_decoder(g)
        for q in range(2):
            flow = exchange(g, q)
            for k in range(10):
                tasks[f"p{g}{q}{k}"] = lambda flow=flow: next(flow)
        ring = Reduce(
            8, z, up, down, lambda b, g=g: dec_prod.at[g, b],
            lambda b, h, g=g: dec_prod.at[g, b, pl.ds(32 * h, 32)],
            [[dr1.at[g, s]] + [drn.at[g, s, i] for i in range(3)] for s in range(2)], dsem2.at[g],
        )
        drains.append(ring)
        tasks[f"D{g}"] = lambda g=g: decoder_product(g)
        for k in range(1, 5):
            tasks[f"r{g}{k}"] = ring.step
        tasks[f"r{g}w"] = lambda g=g, ring=ring: finish_decoder(g, ring)

    sum_y = Gather(*along_y, lambda b: sq_y.at[b], None, sysem)
    sum_x = Gather(*along_x, lambda b: sq_x.at[b], None, sxsem)
    sum_c = remote(sq_c.at[core], sq_c.at[core], scsem.at[0], scsem.at[1], other)
    drains += [sum_y, sum_x]
    tasks["s2"] = sum_y.step
    tasks["s4"] = sum_x.step

    @put("s1")
    def _():
        sq_y[y] = squares[...]
        sum_y.step()

    @put("s3")
    def _():
        sum_y.step()
        sq_x[x] = (sq_y[0] + sq_y[1]) + (sq_y[2] + sq_y[3])
        sum_x.step()

    @put("s5")
    def _():
        sum_x.step()
        sq_c[core] = (sq_x[0] + sq_x[1]) + (sq_x[2] + sq_x[3])
        sum_c.start()

    @put("s6")
    def _():
        sum_c.wait()
        small[z, :, 512:640] = sq_c[0] + sq_c[1]

    def spread(some, c, i):
        terms = [dot(grads[g, c, pl.ds(2 * i, 2)].reshape(384, width), dec_t[g]) for g in some]
        return sum(terms[1:], terms[0])

    def spread_first(i, _):
        back[latent_rows(i // 2, i % 2), :] = spread(range(groups - 1), i // 2, i % 2)
        return 0

    def spread_last(i, total):
        rows = latent_rows(i // 2, i % 2)
        value = back[rows, :] + spread((groups - 1,), i // 2, i % 2)
        value = jnp.where(pre[rows, :] > 0, value, 0.0)
        narrow[rows, :] = value.astype(BF16)
        return total + jnp.sum(value.reshape(48, 8, 512), axis=0)

    tasks["A"] = lambda: lax.fori_loop(0, 4, spread_first, 0)

    @put("B")
    def _():
        small[z, :, 0:512] = lax.fori_loop(0, 4, spread_last, jnp.zeros((8, 512), F32))

    ring_m = Gather(8, z, up, down, lambda b: small.at[b], None, msem)
    drains.append(ring_m)
    for k in range(1, 5):
        tasks[f"b{k}"] = ring_m.step
    keep = []

    @put("bw")
    def _():
        ring_m.step()
        full = ((small[0] + small[1]) + (small[2] + small[3])) + ((small[4] + small[5]) + (small[6] + small[7]))
        sq_out[...] = full[:, 512:640]
        small_sum[...] = full[:, 0:512]
        keep.append(pltpu.make_async_copy(small_sum, bias_out.at[x_hi, core], lsem.at[4]))
        keep[-1].start()
        for i, peer in enumerate(quad_ids):
            copy = remote(small_sum, bias_out.at[x_hi, core], q3sem.at[0, i], q3sem.at[1, i], peer)
            copy.start()
            keep.append(copy)

    def encoder_product(i, side):
        value = dot(res_t[pl.ds(pl.multiple_of(512 * side, 512), 512), :], narrow[...])
        enc_prod[side] = value.astype(BF16).reshape(8, 2, 32, 512)

    def finish_encoder(i, side, ring):
        ring.step()
        esum[side] = enc_prod[side, z].astype(F32) + ern[i, 0, 2].astype(F32) + ern[i, 1, 2].astype(F32)
        for j, (q, peer) in enumerate(zip(quad, quad_ids)):
            if (j == 1) == (i == 1):
                copy = remote(esum.at[q[0], q[1]], enc_out.at[x_hi, core], q2sem.at[0, j], q2sem.at[1, j], peer)
                copy.start()
                keep.append(copy)
        if i == 1:
            keep.append(pltpu.make_async_copy(esum.at[x_hi, core], enc_out.at[x_hi, core], lsem.at[3]))
            keep[-1].start()

    for i, side in enumerate((1 - x_hi, x_hi)):
        ring = Reduce(
            8, z, up, down, lambda b, side=side: enc_prod.at[side, b],
            lambda b, h, side=side: enc_prod.at[side, b, h],
            [[er1.at[i, s]] + [ern.at[i, s, k] for k in range(3)] for s in range(2)], esem2.at[i],
        )
        drains.append(ring)
        tasks[f"E{i}"] = lambda i=i, side=side: encoder_product(i, side)
        for k in range(1, 5):
            tasks[f"q{i}{k}"] = ring.step
        tasks[f"q{i}w"] = lambda i=i, side=side, ring=ring: finish_encoder(i, side, ring)

    for name in ORDER:
        tasks[name]()
    for copy in keep:
        copy.wait()
    for copy in swap + cross:
        copy.wait_send()
    for g in range(groups):
        for i in range(2):
            hand(g, i).wait_send()
    for ring in drains:
        ring.drain()


VM = pl.BlockSpec(memory_space=pltpu.VMEM)


def dmas(*shape):
    return pltpu.SemaphoreType.DMA(shape)


def params(ident):
    return pltpu.CompilerParams(collective_id=ident, has_side_effects=True, vmem_limit_bytes=56 << 20)


def shape(*dims, dtype=BF16):
    return jax.ShapeDtypeStruct(dims, dtype)


def shards(residual, targets, counts, enc_weight, enc_bias, dec_weight):
    loop, dp = lax.axis_index("loop"), lax.axis_index("dp")
    x_hi, core = dp // 16, dp % 2
    enc_quad = enc_weight.reshape(32, 2, 8, 2, 64).transpose(1, 3, 0, 2, 4).reshape(2, 2, 32, 512)
    bias = lax.dynamic_index_in_dim(
        enc_bias.reshape(2, 8, 2, 64).transpose(0, 2, 1, 3).reshape(4, 512), x_hi * 2 + core, 0, True
    )
    n = GROUPS
    width = 2048 // n
    wide, thin = width // 2, width // 4
    goal = lax.dynamic_slice_in_dim(targets, loop * 48, 48, 0).reshape(48, n, width).transpose(1, 0, 2)
    rows = loop * 48 + lax.iota(jnp.int32, 48)
    valid = jnp.broadcast_to((rows < counts[0]).astype(F32)[:, None], (48, 128))
    total_rows = 32 * 384 // 2
    vm = pltpu.VMEM
    dec_grad, enc_grad, bias_grad, sq = pl.pallas_call(
        lambda *refs: step_kernel(n, 2.0 / math.sqrt(total_rows), *refs),
        out_shape=(
            shape(n, 64, width, dtype=F32), shape(2, 2, 32, 512, dtype=F32),
            shape(2, 2, 8, 512, dtype=F32), shape(8, 128, dtype=F32),
        ),
        in_specs=[pl.BlockSpec(memory_space=pl.ANY)] * 3 + [VM] * 3,
        out_specs=(VM,) * 4,
        scratch_shapes=[
            vm((2, 2, 384, 1024), BF16), vm((2, 8, 2, 32, 512), BF16), vm((n, 8, 64, width), BF16),
            vm((1536, 512), F32), vm((1536, 512), BF16), vm((512, 1536), BF16), vm((1024, 1536), BF16),
            vm((n, width, 512), BF16),
            vm((n, 4, 4, 48, width), BF16), vm((n, 4, 4, 48, width), BF16), vm((n, 4, 4, 48, width), BF16),
            vm((n, 2, 4, 4, 48, width), BF16),
            vm((n, 2, 2, 2, 48, wide), BF16), vm((n, 2, 2, 4, 48, wide), BF16),
            vm((n, 2, 2, 48, thin), BF16), vm((n, 2, 2, 48, wide), BF16), vm((n, 2, 4, 48, wide), BF16),
            vm((1536, 512), F32), vm((1536, 512), BF16),
            vm((n, 8, 64, width), BF16), vm((2, 8, 2, 32, 512), BF16),
            vm((n, 2, 32, width), BF16), vm((n, 2, 3, 64, width), BF16),
            vm((2, 2, 32, 512), BF16), vm((2, 2, 3, 2, 32, 512), BF16), vm((2, 2, 32, 512), F32),
            vm((8, 128), F32), vm((4, 8, 128), F32), vm((4, 8, 128), F32), vm((2, 8, 128), F32),
            vm((8, 8, 640), F32), vm((8, 512), F32),
            dmas(2, 2, 2), dmas(2, 2, 2), dmas(2, 2, 2, 2), dmas(2, 2, 2), dmas(2, 2, 4), dmas(n, 2, 2, 4),
            dmas(2, 3), dmas(2, 2), dmas(5), dmas(n, 2, 2), dmas(n, 2, 4, 2, 2, 2), dmas(n, 2, 2, 4),
            dmas(2, 2, 2), dmas(2, 2, 2), dmas(2), dmas(n, 2, 2, 4), dmas(2, 2, 2, 4), dmas(2, 2, 4),
            dmas(2, 3), dmas(2, 3),
        ],
        compiler_params=params(1),
    )(residual, enc_quad, dec_weight.reshape(64, n, width).transpose(1, 0, 2), bias, goal, valid)
    mean_error = jnp.sum(sq) / (total_rows * 2048)
    enc_grad = enc_grad.reshape(2, 2, 32, 8, 64).transpose(2, 0, 3, 1, 4).reshape(32, 2048)
    bias_grad = jnp.sum(bias_grad, axis=2).reshape(2, 2, 8, 64).transpose(0, 2, 1, 3).reshape(2048)
    return mean_error, enc_grad, bias_grad, dec_grad.transpose(1, 0, 2).reshape(64, 2, 1024)


def solution(mesh):
    placed = (
        P("dp", "loop"),
        P("dp", None, None),
        P("dp"),
        P("dp", "loop"),
        P("loop"),
        P(("loop", "dp"), None, None),
    )
    return jax.shard_map(
        shards,
        mesh=mesh,
        in_specs=placed,
        out_specs=(P(), P("dp", "loop"), P("loop"), P(("loop", "dp"), None, None)),
        check_vma=False,
    )
```

time: 620 us -> 147 us (0.24)
  waiting for transfers between devices: 437 us -> 0 us
  Pallas kernels: 0 us -> 130 us
  blocking collectives: 99 us -> 0 us
  matrix products: 34.8 us -> 0 us
  local copies, waits for them, and re-layouts: 24.8 us -> 11 us
  between operations: 16.3 us -> 3.3 us
    all_gather x2 -> x0, waiting for transfers between devices: 162 us -> none  [the longest x1 95.9 us: shards(): decoder = lax.all_gather(dec_weight, 'dp', axis=0, tiled=True)]
    reduce_scatter x1 -> x0, waiting for transfers between devices: 155 us -> none  [shards(): lax.psum_scatter(product.reshape(lax.axis_size('dp') * dec_weight.shape[0...]
    pallas_call x0 -> x1, Pallas kernels: none -> 130 us  [shards(): pl.pallas_call(lambda *refs: step_kernel(n, 2.0 / math.sqrt(total_rows),...]
    psum x1 -> x0, waiting for transfers between devices: 75.8 us -> none  [shards(): lax.psum(partial_value.astype(jnp.bfloat16), 'loop').astype(jnp.float32)]
    psum x1 -> x0, blocking collectives: 72.6 us -> none  [shards(): sq_total = lax.psum(jnp.sum(misfit * misfit), 'dp')]
    unnamed x6 -> x0, waiting for transfers between devices: 45.4 us -> none
    dot_general x5 -> x0, matrix products: 34.8 us -> none  [the longest x1 9.06 us: shards(): jnp.dot(active, dec_flat, preferred_element_type=jnp.float32)]
    all_gather x1 -> x0, blocking collectives: 26.4 us -> none  [shards(): features_all = lax.all_gather(residual, 'loop', axis=1, tiled=True)]
  transfers between devices with their start and end apart: 5 -> 0, of which waited for: 5 -> 0; matrix products, arithmetic and copies ran while one was open for 3% -> 0% of each run, Pallas kernels for 0% -> 0%
where the time goes in v3:
time: 147 us
  Pallas kernels  130 us (88%)
  local copies, waits for them, and re-layouts  11 us (7%)
  between operations  3.3 us (2%)
  other arithmetic  2.22 us (2%)
    pallas_call x1, Pallas kernels, shards(): pl.pallas_call(lambda *refs: step_kernel(n, 2.0 / math.sqrt(total_rows),...  130 us

profile of v3, /device:TPU:1, one launch (start us, length us, event | category | flops | bytes accessed | tf_op | source)
XLA Modules:
  0.0 146.6 jit_solution(14104406605776566485)
XLA Ops:
  0.6 0.0 copy-start
  0.6 0.0 copy-start.2
  1.5 0.8 reshape.50
  2.3 0.1 reshape.51
  2.3 0.6 constant_dynamic-slice_fusion.1.refs_3_
  2.9 0.7 broadcast_in_dim.2.refs_5_
  3.6 0.0 copy-done
  3.6 0.1 constant_dynamic-slice_fusion
  3.7 0.1 reshape.52
  3.8 0.7 copy.30
  4.5 1.2 reshape.47
  5.7 0.9 reshape.48.refs_1_
  6.6 0.0 copy-done.2
  6.6 0.1 reshape.49
  6.7 0.7 copy.28
  7.4 130.1 %shard_map.93 = (f32[4,64,512]{2,1,0:T(8,128)}, f32[2,2,32,512]{3,2,1,0:T(8,128)}, f32[2,2,8,512]{3,2,1,0:T(8,128)}, f32[8,128]{1,0:T(8,128)}) custom-call(bf16[384,128]{1,0:T(8,128)(2,1)} %refs_0_.1, bf16[2,2,32,512]{3,2,1,0:T(8,128)(2,1)} %reshape.48.refs_1_, bf16[4,64,512]{2,1,0:T(8,128)(2,1)} %bitcast.23, f32[1,512]{1,0:T(1,128)} %constant_dynamic-slice_fusion.1.refs_3_, ...), custom_call_target="tpu_custom_call" | custom-call | tf_op jit(solution)/shard_map/pallas_call | solution.py:549
  137.5 0.0 copy-start.1
  137.5 1.3 reduce_sum.18
  139.5 0.9 reduce_sum.19
  140.4 0.1 reshape.55
  140.5 0.7 reshape.56
  141.2 1.1 reshape.53
  142.3 0.4 copy.22
  142.7 1.2 reshape.54
  143.9 0.0 copy-done.1
  143.9 0.3 copy.24
  144.2 1.3 reshape.57
  (4 shorter events, 0.1 us)
Async XLA Ops:
  0.6 3.0 %copy-start = (bf16[384,2,1024]{2,1,0:T(2,128)(2,1)S(1)}, bf16[384,2,1024]{2,1,0:T(2,128)(2,1)}, u32[]{:S(2)}) copy-start(bf16[384,2,1024]{2,1,0:T(2,128)(2,1)} %param.7) | copy-start | bytes 4718596
  0.6 5.9 %copy-start.2 = (bf16[64,2,1024]{2,1,0:T(2,128)(2,1)S(1)}, bf16[64,2,1024]{2,1,0:T(2,128)(2,1)}, u32[]{:S(2)}) copy-start(bf16[64,2,1024]{2,1,0:T(2,128)(2,1)} %param.11) | copy-start | bytes 786436
  137.5 6.3 %copy-start.1 = (f32[4,64,512]{2,1,0:T(8,128)S(1)}, f32[4,64,512]{2,1,0:T(8,128)}, u32[]{:S(2)}) copy-start(f32[4,64,512]{2,1,0:T(8,128)} %get-tuple-element.11) | copy-start | bytes 1572868

commit v4 on v3

--- a/solution.py
+++ b/solution.py
@@ -129,8 +129,8 @@
 
 
 def step_kernel(
-    groups, scale, res, enc, dec, bias, goal, valid, dec_out, enc_out, bias_out, sq_out,
-    res_all, enc_all, dec_all, pre, active, act_t, res_t, dec_t, sent, crossed, mine, grads,
+    groups, total_rows, counts, res, enc_in, dec, bias_in, goal, dec_out, enc_grad, bias_grad, loss,
+    enc, bias, enc_out, bias_out, res_all, enc_all, dec_all, pre, active, act_t, res_t, dec_t, sent, crossed, mine, grads,
     far1, far2, near1, near2, mid, back, narrow, dec_prod, enc_prod,
     dr1, drn, er1, ern, esum, squares, sq_y, sq_x, sq_c, small, small_sum,
     usem, vsem, ysem, xsem, esem, dsem, qsem, csem, lsem, psem, bsem, osem, sysem, sxsem, scsem,
@@ -138,6 +138,7 @@
 ):
     width = 2048 // groups
     wide, thin = width // 2, width // 4
+    scale = 2.0 / math.sqrt(total_rows)
     x, y, z, core = place()
     x_hi = x // 2
     up, down = ident(x, y, (z + 1) % 8, core), ident(x, y, (z + 7) % 8, core)
@@ -162,13 +163,24 @@
     def feature_both(rows, k, yy):
         return res_all.at[core, :, rows, cols(k * 4 + yy, 128)]
 
-    local = [
-        pltpu.make_async_copy(res, feature(pl.ds(0, 384), x, y), lsem.at[0]),
-        pltpu.make_async_copy(enc.at[x_hi, core], enc_all.at[x_hi, z, core], lsem.at[1]),
-        pltpu.make_async_copy(dec, dec_all.at[:, z], lsem.at[2]),
-    ]
+    def column(g):
+        return divmod(g * width, 1024)
+
+    local = [pltpu.make_async_copy(res, feature(pl.ds(0, 384), x, y), lsem.at[0])]
+    for g in range(groups):
+        t, at = column(g)
+        local.append(pltpu.make_async_copy(dec.at[t, :, pl.ds(at, width)], dec_all.at[g, z], lsem.at[2 + g]))
     for copy in local:
         copy.start()
+    runs = [(h, c, k, 1024 * h + 128 * k + 64 * c) for h in range(2) for c in range(2) for k in range(8)]
+    for h, c, k, at in runs:
+        enc[h, c, :, 64 * k : 64 * k + 64] = enc_in[:, at : at + 64]
+    local.append(pltpu.make_async_copy(enc.at[x_hi, core], enc_all.at[x_hi, z, core], lsem.at[1]))
+    local[-1].start()
+    both = bias_in[pl.ds(pl.multiple_of(8 * x_hi, 8), 8), :]
+    chosen = jnp.where(core == 0, both[:, 0:64], both[:, 64:128])
+    for k in range(8):
+        bias[:, 64 * k : 64 * k + 64] = chosen[k : k + 1, :]
     greet([up, down, east, west, north, south] + quad_ids)
     swap = []
     for i, (q, peer) in enumerate(zip(quad, quad_ids)):
@@ -293,12 +305,14 @@
 
         lax.fori_loop(0, 2, one, 0)
 
-    ok = valid[:, 0:1]
+    row = ((x % 2) * 4 + y) * 48 + lax.broadcasted_iota(jnp.int32, (48, 128), 0)
+    ok = (row < counts[0]).astype(F32)[:, 0:1]
     along_x, along_y = (4, x, east, west), (4, y, north, south)
     squares[...] = jnp.zeros_like(squares)
 
     def exchange(g, q):
         own, out = mine.at[g], grads.at[g, core]
+        t, start = column(g)
         w = pl.ds(q * wide, wide)
         first, then = (along_x, along_y) if q == 0 else (along_y, along_x)
         at, near = first[1], then[1]
@@ -349,7 +363,7 @@
         yield
         red_near.step()
         rebuilt = mid[g, q, near].astype(F32) + near2[g, q, 0].astype(F32) + near2[g, q, 1].astype(F32)
-        miss = (rebuilt - goal[g, :, w].astype(F32)) * ok
+        miss = (rebuilt - goal[t, :, pl.ds(start + q * wide, wide)].astype(F32)) * ok
         cell(near, w)[...] = (scale * miss).astype(BF16)
         ring_near.step()
         square = miss * miss
@@ -385,7 +399,8 @@
 
     def finish_decoder(g, ring):
         ring.step()
-        dec_out[g] = dec_prod[g, z].astype(F32) + drn[g, 0, 2].astype(F32) + drn[g, 1, 2].astype(F32)
+        t, at = column(g)
+        dec_out[t, :, at : at + width] = dec_prod[g, z].astype(F32) + drn[g, 0, 2].astype(F32) + drn[g, 1, 2].astype(F32)
 
     for g in range(groups):
         tasks[f"o{g}"] = lambda g=g: decode_other(g)
@@ -466,9 +481,9 @@
     def _():
         ring_m.step()
         full = ((small[0] + small[1]) + (small[2] + small[3])) + ((small[4] + small[5]) + (small[6] + small[7]))
-        sq_out[...] = full[:, 512:640]
+        loss[0] = jnp.sum(full[:, 512:640]) / (total_rows * 2048)
         small_sum[...] = full[:, 0:512]
-        keep.append(pltpu.make_async_copy(small_sum, bias_out.at[x_hi, core], lsem.at[4]))
+        keep.append(pltpu.make_async_copy(small_sum, bias_out.at[x_hi, core], lsem.at[2 + groups]))
         keep[-1].start()
         for i, peer in enumerate(quad_ids):
             copy = remote(small_sum, bias_out.at[x_hi, core], q3sem.at[0, i], q3sem.at[1, i], peer)
@@ -488,7 +503,7 @@
                 copy.start()
                 keep.append(copy)
         if i == 1:
-            keep.append(pltpu.make_async_copy(esum.at[x_hi, core], enc_out.at[x_hi, core], lsem.at[3]))
+            keep.append(pltpu.make_async_copy(esum.at[x_hi, core], enc_out.at[x_hi, core], lsem.at[3 + groups]))
             keep[-1].start()
 
     for i, side in enumerate((1 - x_hi, x_hi)):
@@ -507,6 +522,10 @@
         tasks[name]()
     for copy in keep:
         copy.wait()
+    sums = [[jnp.sum(bias_out[h, c], axis=0, keepdims=True) for c in range(2)] for h in range(2)]
+    for h, c, k, at in runs:
+        enc_grad[:, at : at + 64] = enc_out[h, c, :, 64 * k : 64 * k + 64]
+        bias_grad[8 * h + k : 8 * h + k + 1, 64 * c : 64 * c + 64] = sums[h][c][:, 64 * k : 64 * k + 64]
     for copy in swap + cross:
         copy.wait_send()
     for g in range(groups):
@@ -531,30 +550,25 @@
     return jax.ShapeDtypeStruct(dims, dtype)
 
 
+SM = pl.BlockSpec(memory_space=pltpu.SMEM)
+
+
 def shards(residual, targets, counts, enc_weight, enc_bias, dec_weight):
-    loop, dp = lax.axis_index("loop"), lax.axis_index("dp")
-    x_hi, core = dp // 16, dp % 2
-    enc_quad = enc_weight.reshape(32, 2, 8, 2, 64).transpose(1, 3, 0, 2, 4).reshape(2, 2, 32, 512)
-    bias = lax.dynamic_index_in_dim(
-        enc_bias.reshape(2, 8, 2, 64).transpose(0, 2, 1, 3).reshape(4, 512), x_hi * 2 + core, 0, True
-    )
     n = GROUPS
     width = 2048 // n
     wide, thin = width // 2, width // 4
-    goal = lax.dynamic_slice_in_dim(targets, loop * 48, 48, 0).reshape(48, n, width).transpose(1, 0, 2)
-    rows = loop * 48 + lax.iota(jnp.int32, 48)
-    valid = jnp.broadcast_to((rows < counts[0]).astype(F32)[:, None], (48, 128))
+    goal = lax.dynamic_slice_in_dim(targets, lax.axis_index("loop") * 48, 48, 0).transpose(1, 0, 2)
     total_rows = 32 * 384 // 2
     vm = pltpu.VMEM
-    dec_grad, enc_grad, bias_grad, sq = pl.pallas_call(
-        lambda *refs: step_kernel(n, 2.0 / math.sqrt(total_rows), *refs),
+    dec_grad, enc_grad, bias_grad, loss = pl.pallas_call(
+        lambda *refs: step_kernel(n, total_rows, *refs),
         out_shape=(
-            shape(n, 64, width, dtype=F32), shape(2, 2, 32, 512, dtype=F32),
-            shape(2, 2, 8, 512, dtype=F32), shape(8, 128, dtype=F32),
+            shape(2, 64, 1024, dtype=F32), shape(32, 2048, dtype=F32), shape(16, 128, dtype=F32), shape(1, dtype=F32),
         ),
-        in_specs=[pl.BlockSpec(memory_space=pl.ANY)] * 3 + [VM] * 3,
-        out_specs=(VM,) * 4,
+        in_specs=[SM, pl.BlockSpec(memory_space=pl.ANY), VM, pl.BlockSpec(memory_space=pl.ANY), VM, VM],
+        out_specs=(VM, VM, VM, SM),
         scratch_shapes=[
+            vm((2, 2, 32, 512), BF16), vm((1, 512), F32), vm((2, 2, 32, 512), F32), vm((2, 2, 8, 512), F32),
             vm((2, 2, 384, 1024), BF16), vm((2, 8, 2, 32, 512), BF16), vm((n, 8, 64, width), BF16),
             vm((1536, 512), F32), vm((1536, 512), BF16), vm((512, 1536), BF16), vm((1024, 1536), BF16),
             vm((n, width, 512), BF16),
@@ -569,16 +583,13 @@
             vm((8, 128), F32), vm((4, 8, 128), F32), vm((4, 8, 128), F32), vm((2, 8, 128), F32),
             vm((8, 8, 640), F32), vm((8, 512), F32),
             dmas(2, 2, 2), dmas(2, 2, 2), dmas(2, 2, 2, 2), dmas(2, 2, 2), dmas(2, 2, 4), dmas(n, 2, 2, 4),
-            dmas(2, 3), dmas(2, 2), dmas(5), dmas(n, 2, 2), dmas(n, 2, 4, 2, 2, 2), dmas(n, 2, 2, 4),
+            dmas(2, 3), dmas(2, 2), dmas(n + 4), dmas(n, 2, 2), dmas(n, 2, 4, 2, 2, 2), dmas(n, 2, 2, 4),
             dmas(2, 2, 2), dmas(2, 2, 2), dmas(2), dmas(n, 2, 2, 4), dmas(2, 2, 2, 4), dmas(2, 2, 4),
             dmas(2, 3), dmas(2, 3),
         ],
         compiler_params=params(1),
-    )(residual, enc_quad, dec_weight.reshape(64, n, width).transpose(1, 0, 2), bias, goal, valid)
-    mean_error = jnp.sum(sq) / (total_rows * 2048)
-    enc_grad = enc_grad.reshape(2, 2, 32, 8, 64).transpose(2, 0, 3, 1, 4).reshape(32, 2048)
-    bias_grad = jnp.sum(bias_grad, axis=2).reshape(2, 2, 8, 64).transpose(0, 2, 1, 3).reshape(2048)
-    return mean_error, enc_grad, bias_grad, dec_grad.transpose(1, 0, 2).reshape(64, 2, 1024)
+    )(counts, residual, enc_weight, dec_weight.transpose(1, 0, 2), enc_bias.reshape(16, 128), goal)
+    return loss.reshape(()), enc_grad, bias_grad.reshape(2048), dec_grad.transpose(1, 0, 2)
 
 
 def solution(mesh):

time: 147 us -> 142 us (0.966)
  local copies, waits for them, and re-layouts: 11 us -> 7.73 us
  other arithmetic: 2.22 us -> 0 us
    reshape x14 -> x0, local copies, waits for them, and re-layouts: 8.83 us -> none  [the longest x2 2.27 us: shards(): enc_grad.reshape(2, 2, 32, 8, 64).transpose(2, 0, 3, 1, 4).reshape(32, 2048)]
    unnamed x6 -> x9, local copies, waits for them, and re-layouts: 0.02 us -> 7.59 us
    reduce_sum x2 -> x0, other arithmetic: 2.22 us -> none  [the longest x1 1.35 us: shards(): mean_error = jnp.sum(sq) / (total_rows * 2048)]
where the time goes in v4:
time: 142 us; the launch traced here: 141 us
  Pallas kernels  131 us (92%)
  local copies, waits for them, and re-layouts  7.73 us (5%)
  between operations  3.2 us (2%)
    pallas_call x1, Pallas kernels, shards(): pl.pallas_call(lambda *refs: step_kernel(n, total_rows, *refs), out_shape...  131 us
    unnamed x9, local copies, waits for them, and re-layouts  7.59 us

profile of v4, /device:TPU:1, one launch (start us, length us, event | category | flops | bytes accessed | tf_op | source)
XLA Modules:
  0.0 141.5 jit_solution(7294117305619892619)
XLA Ops:
  0.6 0.0 copy-start
  1.4 0.6 copy-done
  2.1 0.1 constant_dynamic-slice_fusion
  2.2 0.7 copy.17
  2.9 1.7 %copy.16 = bf16[64,2,1024]{2,0,1:T(8,128)(2,1)} copy(bf16[64,2,1024]{2,1,0:T(2,128)(2,1)} %param.11) | data formatting | bytes 524288 | tf_op args[5]
  4.6 130.6 %shard_map.93 = (f32[2,64,1024]{2,1,0:T(8,128)}, f32[32,2048]{1,0:T(8,128)}, f32[16,128]{1,0:T(8,128)}, f32[1]{0:T(128)}) custom-call(s32[1]{0:T(128)S(6)} %copy.21.refs_0_, bf16[384,128]{1,0:T(8,128)(2,1)} %refs_1_.1, bf16[32,2048]{1,0:T(8,128)(2,1)} %refs_2_.1, bf16[2,64,1024]{2,1,0:T(8,128)(2,1)} %bitcast.10, f32[16,128]{1,0:T(8,128)} %bitcast.13, ...), custom_call_target="tpu_custom_call" | custom-call | tf_op jit(solution)/shard_map/pallas_call | solution.py:563
  135.2 0.0 copy-start.1
  135.2 2.2 %copy.12 = f32[64,2,1024]{2,1,0:T(2,128)} copy(f32[64,2,1024]{2,0,1:T(8,128)} %bitcast.12) | data formatting | bytes 1048576
  138.1 1.7 %copy.23 = f32[32,2048]{1,0:T(8,128)} copy(f32[32,2048]{1,0:T(8,128)} %get-tuple-element.21) | data formatting | bytes 524288
  139.8 0.0 copy-done.1
  139.8 0.6 copy.24
Async XLA Ops:
  0.6 1.4 %copy-start = (bf16[384,2,1024]{2,1,0:T(2,128)(2,1)S(1)}, bf16[384,2,1024]{2,1,0:T(2,128)(2,1)}, u32[]{:S(2)}) copy-start(bf16[384,2,1024]{2,1,0:T(2,128)(2,1)} %param.7) | copy-start | bytes 4718596
  135.2 4.6 %copy-start.1 = (f32[16,128]{1,0:T(8,128)S(1)}, f32[16,128]{1,0:T(8,128)}, u32[]{:S(2)}) copy-start(f32[16,128]{1,0:T(8,128)} %get-tuple-element.10) | copy-start | bytes 24580

commit v5 on v4

--- a/solution.py
+++ b/solution.py
@@ -105,22 +105,22 @@
 
 GROUPS = 4
 ORDER = (
-    "d31", "v1", "u1", "d01", "e1", "d21", "u2", "v2", "d02", "x1", "y1", "e2",
-    "d32", "d11", "x2", "y2", "e3", "d03", "d33", "yw", "xw", "e4", "d12", "d04",
-    "d22", "d34", "rw", "ew", "n0", "d13", "n1", "d0w", "o0", "f0", "d23", "d3w",
-    "o3", "d14", "fl", "f3", "m0", "d24", "p000", "p010", "d1w", "o1", "m3", "p300",
-    "d2w", "o2", "p310", "p001", "p011", "m1", "p100", "p110", "p301", "m2", "p210", "p200",
-    "p311", "p002", "f1", "p012", "p101", "p211", "ff", "p013", "p312", "p201", "p003", "p302",
-    "p111", "p212", "p014", "p102", "p313", "p004", "f2", "p303", "p202", "p213", "p015", "p314",
-    "p103", "p005", "p112", "p203", "p304", "p016", "p315", "p214", "p113", "p006", "p305", "p204",
-    "p104", "p316", "p114", "p215", "p306", "p205", "p017", "s1", "p105", "p007", "p115", "p216",
-    "p206", "p317", "p307", "p018", "p008", "p116", "s2", "p106", "p217", "p019", "p207", "p009",
-    "p318", "D0", "r01", "s3", "p308", "p107", "p319", "p117", "p218", "s4", "r02", "p309",
-    "p208", "D3", "p108", "r31", "p118", "p209", "p219", "D2", "r21", "p109", "r03", "p119",
-    "r32", "s5", "A", "s6", "r22", "r33", "B", "b1", "r23", "r04", "E0", "b2",
-    "q01", "r24", "E1", "b3", "q11", "q02", "D1", "r11", "b4", "r2w", "q12", "q03",
-    "r12", "r0w", "q13", "bw", "q04", "r13", "q14", "r34", "q0w", "r14", "q1w", "r3w",
-    "r1w",
+    "d01", "v1", "u1", "e1", "d11", "v2", "u2", "d02", "e2", "y1", "x1", "d21",
+    "d12", "e3", "x2", "d03", "d31", "y2", "e4", "d13", "d22", "xw", "d04", "d32",
+    "yw", "ew", "n0", "d14", "rw", "n1", "d23", "d0w", "o0", "d33", "f0", "d1w",
+    "o1", "d24", "m0", "p010", "p000", "d34", "m1", "d2w", "o2", "p110", "p100", "p011",
+    "d3w", "p001", "o3", "m2", "p200", "p210", "p101", "p111", "m3", "p012", "p002", "p300",
+    "p310", "p201", "p211", "ff", "p102", "p013", "p003", "p112", "p301", "p311", "f1", "fl",
+    "f3", "p212", "p202", "p103", "p014", "p113", "p004", "f2", "p302", "p312", "p203", "p213",
+    "p104", "p015", "p114", "p005", "p303", "p313", "p204", "p214", "p105", "p016", "p115", "p006",
+    "p304", "p314", "s1", "p205", "p215", "p116", "p106", "p017", "s2", "p007", "p315", "p305",
+    "p216", "p206", "p117", "p107", "p018", "p008", "p316", "p306", "p019", "s3", "p009", "p217",
+    "p207", "p118", "D0", "p108", "p119", "r01", "p317", "p307", "p109", "p218", "D1", "p208",
+    "p219", "r11", "r02", "p318", "p209", "D2", "p308", "r21", "p319", "s4", "r12", "p309",
+    "D3", "r31", "r03", "r22", "A", "r13", "s5", "r32", "B", "s6", "b1", "r23",
+    "E0", "q01", "r04", "E1", "q11", "b2", "q02", "r33", "q12", "b3", "q03", "r24",
+    "q13", "r0w", "q04", "b4", "r2w", "r14", "q14", "q0w", "r34", "bw", "q1w", "r1w",
+    "r3w",
 )
 
 
@@ -249,7 +249,8 @@
     tasks["yw"] = lambda: (ring_y[0].step(), ring_y[1].step(), cross_over(1, low))
     tasks["rw"] = lambda: [copy.wait_recv() for copy in cross]
 
-    def encode(i, _):
+    def encode(k, _):
+        i = (2 * core + k) % 4
         rows = pl.ds(pl.multiple_of(384 * i, 384), 384)
         value = dot(res_all[i // 2, i % 2], enc_all[...].reshape(1024, 512)) + bias[...]
         pre[rows, :] = value
@@ -390,12 +391,8 @@
         yield
 
     def decoder_product(g):
-        def one(i, _):
-            value = dot(act_t[...], grads[g, :, :, :, :, cols(i, 256)].reshape(1536, 256))
-            dec_prod[g, :, :, cols(i, 256)] = value.astype(BF16).reshape(8, 64, 256)
-            return 0
-
-        lax.fori_loop(0, width // 256, one, 0)
+        value = dot(act_t[...], grads[g].reshape(1536, width))
+        dec_prod[g] = value.astype(BF16).reshape(8, 64, width)
 
     def finish_decoder(g, ring):
         ring.step()

time: 142 us -> 139 us (0.979)
  Pallas kernels: 131 us -> 128 us
    pallas_call x1, Pallas kernels: 131 us -> 128 us  [shards(): pl.pallas_call(lambda *refs: step_kernel(n, total_rows, *refs), out_shape...]
where the time goes in v5:
time: 139 us
  Pallas kernels  128 us (92%)
  local copies, waits for them, and re-layouts  7.73 us (6%)
  between operations  3.2 us (2%)
    pallas_call x1, Pallas kernels, shards(): pl.pallas_call(lambda *refs: step_kernel(n, total_rows, *refs), out_shape...  128 us
    unnamed x9, local copies, waits for them, and re-layouts  7.59 us

profile of v5, /device:TPU:1, one launch (start us, length us, event | category | flops | bytes accessed | tf_op | source)
XLA Modules:
  0.0 138.6 jit_solution(6990257118025862640)
XLA Ops:
  0.6 0.0 copy-start
  1.4 0.6 copy-done
  2.1 0.1 constant_dynamic-slice_fusion
  2.2 0.7 copy.17
  2.9 1.7 %copy.16 = bf16[64,2,1024]{2,0,1:T(8,128)(2,1)} copy(bf16[64,2,1024]{2,1,0:T(2,128)(2,1)} %param.11) | data formatting | bytes 524288 | tf_op args[5]
  4.6 127.6 %shard_map.93 = (f32[2,64,1024]{2,1,0:T(8,128)}, f32[32,2048]{1,0:T(8,128)}, f32[16,128]{1,0:T(8,128)}, f32[1]{0:T(128)}) custom-call(s32[1]{0:T(128)S(6)} %copy.21.refs_0_, bf16[384,128]{1,0:T(8,128)(2,1)} %refs_1_.1, bf16[32,2048]{1,0:T(8,128)(2,1)} %refs_2_.1, bf16[2,64,1024]{2,1,0:T(8,128)(2,1)} %bitcast.10, f32[16,128]{1,0:T(8,128)} %bitcast.13, ...), custom_call_target="tpu_custom_call" | custom-call | tf_op jit(solution)/shard_map/pallas_call | solution.py:560
  132.3 0.0 copy-start.1
  132.3 2.2 %copy.12 = f32[64,2,1024]{2,1,0:T(2,128)} copy(f32[64,2,1024]{2,0,1:T(8,128)} %bitcast.12) | data formatting | bytes 1048576
  135.2 1.7 %copy.23 = f32[32,2048]{1,0:T(8,128)} copy(f32[32,2048]{1,0:T(8,128)} %get-tuple-element.21) | data formatting | bytes 524288
  136.8 0.0 copy-done.1
  136.8 0.6 copy.24
Async XLA Ops:
  0.6 1.4 %copy-start = (bf16[384,2,1024]{2,1,0:T(2,128)(2,1)S(1)}, bf16[384,2,1024]{2,1,0:T(2,128)(2,1)}, u32[]{:S(2)}) copy-start(bf16[384,2,1024]{2,1,0:T(2,128)(2,1)} %param.7) | copy-start | bytes 4718596
  132.3 4.6 %copy-start.1 = (f32[16,128]{1,0:T(8,128)S(1)}, f32[16,128]{1,0:T(8,128)}, u32[]{:S(2)}) copy-start(f32[16,128]{1,0:T(8,128)} %get-tuple-element.10) | copy-start | bytes 24580

commit v6 on v5

--- a/solution.py
+++ b/solution.py
@@ -26,7 +26,7 @@
     barrier = pltpu.get_barrier_semaphore()
     for peer in peers:
         pl.semaphore_signal(barrier, inc=1, device_id=peer, device_id_type=MESH)
-    pl.semaphore_wait(barrier, len(peers))
+    return lambda: pl.semaphore_wait(barrier, len(peers))
 
 
 def remote(src, dst, send, recv, peer):
@@ -105,22 +105,22 @@
 
 GROUPS = 4
 ORDER = (
-    "d01", "v1", "u1", "e1", "d11", "v2", "u2", "d02", "e2", "y1", "x1", "d21",
-    "d12", "e3", "x2", "d03", "d31", "y2", "e4", "d13", "d22", "xw", "d04", "d32",
-    "yw", "ew", "n0", "d14", "rw", "n1", "d23", "d0w", "o0", "d33", "f0", "d1w",
-    "o1", "d24", "m0", "p010", "p000", "d34", "m1", "d2w", "o2", "p110", "p100", "p011",
-    "d3w", "p001", "o3", "m2", "p200", "p210", "p101", "p111", "m3", "p012", "p002", "p300",
-    "p310", "p201", "p211", "ff", "p102", "p013", "p003", "p112", "p301", "p311", "f1", "fl",
-    "f3", "p212", "p202", "p103", "p014", "p113", "p004", "f2", "p302", "p312", "p203", "p213",
-    "p104", "p015", "p114", "p005", "p303", "p313", "p204", "p214", "p105", "p016", "p115", "p006",
-    "p304", "p314", "s1", "p205", "p215", "p116", "p106", "p017", "s2", "p007", "p315", "p305",
-    "p216", "p206", "p117", "p107", "p018", "p008", "p316", "p306", "p019", "s3", "p009", "p217",
-    "p207", "p118", "D0", "p108", "p119", "r01", "p317", "p307", "p109", "p218", "D1", "p208",
-    "p219", "r11", "r02", "p318", "p209", "D2", "p308", "r21", "p319", "s4", "r12", "p309",
-    "D3", "r31", "r03", "r22", "A", "r13", "s5", "r32", "B", "s6", "b1", "r23",
-    "E0", "q01", "r04", "E1", "q11", "b2", "q02", "r33", "q12", "b3", "q03", "r24",
-    "q13", "r0w", "q04", "b4", "r2w", "r14", "q14", "q0w", "r34", "bw", "q1w", "r1w",
-    "r3w",
+    "d01", "u1", "v1", "e1", "d21", "v2", "u2", "d02", "e2", "d11", "x1", "y1",
+    "d03", "e3", "d12", "x2", "d31", "y2", "e4", "xw", "d13", "d22", "yw", "d04",
+    "d32", "ew", "n0", "rw", "d14", "n1", "d23", "d0w", "o0", "f0", "d33", "d1w",
+    "o1", "d24", "m0", "p010", "p000", "d34", "m1", "p110", "d2w", "p100", "o2", "p011",
+    "p001", "d3w", "o3", "p111", "p101", "m2", "p200", "p210", "m3", "p310", "p300", "p002",
+    "p012", "p112", "p102", "p211", "p201", "ff", "p003", "p013", "p311", "p301", "f1", "p103",
+    "p113", "f2", "p212", "p202", "p014", "p004", "fl", "p312", "p302", "p203", "p114", "p104",
+    "p015", "p213", "p005", "p313", "p303", "p204", "p115", "p105", "p016", "p214", "p006", "p304",
+    "p314", "p116", "s1", "p106", "f3", "p017", "p215", "p205", "p007", "p315", "p305", "s2",
+    "p117", "p107", "p018", "p216", "p206", "p306", "p008", "p019", "p316", "s3", "p118", "p108",
+    "p009", "D0", "r01", "p119", "p109", "p217", "D1", "p207", "r11", "p317", "r02", "A",
+    "r12", "p208", "p218", "p307", "s4", "p318", "r03", "p209", "p219", "D2", "r21", "r13",
+    "p319", "p308", "C", "r04", "p309", "r22", "B", "r14", "s5", "E0", "q01", "s6",
+    "b1", "r23", "E1", "q11", "q02", "b2", "D3", "r31", "q12", "r0w", "r1w", "q03",
+    "b3", "r32", "q13", "q04", "r33", "b4", "q14", "r24", "q0w", "r34", "q1w", "bw",
+    "r2w", "r3w",
 )
 
 
@@ -147,6 +147,7 @@
     other = ident(x, y, z, 1 - core)
     quad = [(1 - x_hi, core), (x_hi, 1 - core), (1 - x_hi, 1 - core)]
     quad_ids = [ident((x + 2) % 4, y, z, core), other, ident((x + 2) % 4, y, z, 1 - core)]
+    all_here = greet([up, down, east, west, north, south] + quad_ids)
     drains = []
 
     def cols(block, width):
@@ -181,7 +182,7 @@
     chosen = jnp.where(core == 0, both[:, 0:64], both[:, 64:128])
     for k in range(8):
         bias[:, 64 * k : 64 * k + 64] = chosen[k : k + 1, :]
-    greet([up, down, east, west, north, south] + quad_ids)
+    all_here()
     swap = []
     for i, (q, peer) in enumerate(zip(quad, quad_ids)):
         copy = remote(enc.at[q[0], q[1]], enc_all.at[x_hi, z, core], qsem.at[0, i], qsem.at[1, i], peer)
@@ -452,7 +453,11 @@
         return sum(terms[1:], terms[0])
 
     def spread_first(i, _):
-        back[latent_rows(i // 2, i % 2), :] = spread(range(groups - 1), i // 2, i % 2)
+        back[latent_rows(i // 2, i % 2), :] = spread(range(groups - 2), i // 2, i % 2)
+        return 0
+
+    def spread_next(i, _):
+        back[latent_rows(i // 2, i % 2), :] += spread((groups - 2,), i // 2, i % 2)
         return 0
 
     def spread_last(i, total):
@@ -463,6 +468,7 @@
         return total + jnp.sum(value.reshape(48, 8, 512), axis=0)
 
     tasks["A"] = lambda: lax.fori_loop(0, 4, spread_first, 0)
+    tasks["C"] = lambda: lax.fori_loop(0, 4, spread_next, 0)
 
     @put("B")
     def _():

time: 139 us -> 138 us (level)
  no operation moved by 1% of the time
where the time goes in v6:
time: 138 us
  Pallas kernels  127 us (92%)
  local copies, waits for them, and re-layouts  7.73 us (6%)
  between operations  3.2 us (2%)
    pallas_call x1, Pallas kernels, shards(): pl.pallas_call(lambda *refs: step_kernel(n, total_rows, *refs), out_shape...  127 us
    unnamed x9, local copies, waits for them, and re-layouts  7.59 us

profile of v6, /device:TPU:1, one launch (start us, length us, event | category | flops | bytes accessed | tf_op | source)
XLA Modules:
  0.0 138.2 jit_solution(1840762849774885252)
XLA Ops:
  0.6 0.0 copy-start
  1.4 0.6 copy-done
  2.1 0.1 constant_dynamic-slice_fusion
  2.2 0.7 copy.17
  2.9 1.7 %copy.16 = bf16[64,2,1024]{2,0,1:T(8,128)(2,1)} copy(bf16[64,2,1024]{2,1,0:T(2,128)(2,1)} %param.11) | data formatting | bytes 524288 | tf_op args[5]
  4.6 127.3 %shard_map.93 = (f32[2,64,1024]{2,1,0:T(8,128)}, f32[32,2048]{1,0:T(8,128)}, f32[16,128]{1,0:T(8,128)}, f32[1]{0:T(128)}) custom-call(s32[1]{0:T(128)S(6)} %copy.21.refs_0_, bf16[384,128]{1,0:T(8,128)(2,1)} %refs_1_.1, bf16[32,2048]{1,0:T(8,128)(2,1)} %refs_2_.1, bf16[2,64,1024]{2,1,0:T(8,128)(2,1)} %bitcast.10, f32[16,128]{1,0:T(8,128)} %bitcast.13, ...), custom_call_target="tpu_custom_call" | custom-call | tf_op jit(solution)/shard_map/pallas_call | solution.py:566
  131.9 0.0 copy-start.1
  131.9 2.2 %copy.12 = f32[64,2,1024]{2,1,0:T(2,128)} copy(f32[64,2,1024]{2,0,1:T(8,128)} %bitcast.12) | data formatting | bytes 1048576
  134.8 1.7 %copy.23 = f32[32,2048]{1,0:T(8,128)} copy(f32[32,2048]{1,0:T(8,128)} %get-tuple-element.21) | data formatting | bytes 524288
  136.5 0.0 copy-done.1
  136.5 0.6 copy.24
Async XLA Ops:
  0.6 1.4 %copy-start = (bf16[384,2,1024]{2,1,0:T(2,128)(2,1)S(1)}, bf16[384,2,1024]{2,1,0:T(2,128)(2,1)}, u32[]{:S(2)}) copy-start(bf16[384,2,1024]{2,1,0:T(2,128)(2,1)} %param.7) | copy-start | bytes 4718596
  131.9 4.6 %copy-start.1 = (f32[16,128]{1,0:T(8,128)S(1)}, f32[16,128]{1,0:T(8,128)}, u32[]{:S(2)}) copy-start(f32[16,128]{1,0:T(8,128)} %get-tuple-element.10) | copy-start | bytes 24580
